TPU v7x, 256 devices: a whole 4x4x8 slice. The times are simulated.
256 devices in a mesh: member: 4 (over x), tile: 64 (over z, y, core).
Axes of the slice: x: 4, y: 4, z: 8, core: 2. Of those that a mesh axis runs over, the one named last changes fastest.
Arguments:
- member_state: float32 [40, 16, 1536, 128], P('member', None, 'tile'), may hold values from -6 to 6
- courant: float32 [2, 16, 1536, 128], P(None, None, 'tile'), may hold values from -0.45 to 0.45
- obs_col: int32 [131072], P(('member', 'tile')), may hold values from 0 to 767
- obs_lev: int32 [131072], P(('member', 'tile')), may hold values from 0 to 15
- innovation: float32 [131072], P(('member', 'tile')), may hold values from -24 to 24
- obs_var: float32 [131072], P(('member', 'tile')), may hold values from 0.5 to 4
- mode_waves: int32 [12], replicated, may hold values from 0 to 15
Outputs:
- advanced: float32 [40, 16, 1536, 128], P('member', None, 'tile')
- increment: float32 [16, 196608], P(None, ('member', 'tile'))
All inputs are finite; a program needn't handle non-finite values.
Results may differ from a plain program's by a relative error of at most 0.0003.
Values sent between devices are 32-bit elements; how exact they have to be, the bound alone decides.
A program may use at most 128 MiB of HBM per device.

v0:
```python
import jax
import jax.numpy as jnp
from jax import lax
from jax.sharding import PartitionSpec as P


def extended(cells, sides, width):
    for axis, dim in sides:
        count = lax.axis_size(axis)
        head = lax.slice_in_dim(cells, 0, width, axis=dim)
        tail = lax.slice_in_dim(cells, cells.shape[dim] - width, cells.shape[dim], axis=dim)
        cells = jnp.concatenate(
            [
                lax.ppermute(tail, axis, [(i, (i + 1) % count) for i in range(count)]),
                cells,
                lax.ppermute(head, axis, [((i + 1) % count, i) for i in range(count)]),
            ],
            axis=dim,
        )
    return cells


def upwind(padded, courant):
    centre = padded[:, :, 1:-1]
    west = padded[:, :, :-2]
    east = padded[:, :, 2:]
    south = jnp.roll(centre, 1, axis=3)
    north = jnp.roll(centre, -1, axis=3)
    along_x = courant[0]
    along_y = courant[1]
    return (
        centre
        - jnp.maximum(along_x, 0.0) * (centre - west)
        - jnp.minimum(along_x, 0.0) * (east - centre)
        - jnp.maximum(along_y, 0.0) * (centre - south)
        - jnp.minimum(along_y, 0.0) * (north - centre)
    )


def mode_profiles(mode_waves, levels, count):
    heights = jnp.arange(levels).astype(jnp.float32)
    waves = mode_waves.astype(jnp.float32)
    scales = 1.0 / jnp.sqrt(1.0 + jnp.arange(count).astype(jnp.float32))
    return scales[:, None] * jnp.cos(jnp.pi * waves[:, None] * (heights[None, :] + 0.5) / levels)


def on_device(member_state, courant, obs_col, obs_lev, innovation, obs_var, mode_waves):
    highest = lax.Precision.HIGHEST
    mem_local, levels, cols_x, cols_y = member_state.shape
    groups = lax.axis_size("member")
    field = member_state
    for passes in range(2):
        padded = extended(field, (("tile", 2),), 1)
        field = upwind(padded, courant)
    tile_cols = cols_x * cols_y
    flat_state = field.reshape(mem_local, levels, tile_cols)
    total = mem_local * groups
    owned_cols = tile_cols // groups
    norm_root = jnp.sqrt(jnp.float32(total - 1))
    owned = lax.all_to_all(flat_state, "member", split_axis=2, concat_axis=0, tiled=True)
    anomaly = (owned - jnp.mean(owned, axis=0, keepdims=True)) / norm_root
    flat_index = obs_lev * owned_cols + obs_col
    picked = jnp.take(anomaly.reshape(total, levels * owned_cols), flat_index, axis=1)
    count = mode_waves.shape[0]
    profiles = mode_profiles(mode_waves, levels, count)
    weighted = picked / obs_var[None, :]
    width = total * count

    def level_terms(level):
        masked = weighted * (obs_lev == level).astype(jnp.float32)[None, :]
        return (
            jnp.dot(masked, picked.T, precision=highest),
            jnp.dot(masked, innovation, precision=highest),
        )

    sums, cross = lax.map(level_terms, jnp.arange(levels))
    sums, cross = lax.psum((sums, cross), ("member", "tile"))
    gram_sum = jnp.einsum("lkm,jl,il->kjmi", sums, profiles, profiles, precision=highest).reshape(
        width, width
    )
    rhs = jnp.einsum("lk,jl->kj", cross, profiles, precision=highest).reshape(width)
    system = jnp.eye(width, dtype=jnp.float32) + gram_sum
    factor = jnp.linalg.cholesky(system)
    weights = jax.scipy.linalg.cho_solve((factor, True), rhs)
    coeffs = jnp.dot(weights.reshape(total, count), profiles, precision=highest)
    increment = jnp.einsum("klc,kl->lc", anomaly, coeffs, precision=highest)
    return (field, increment)


def solution(mesh):
    in_specs = (
        P("member", None, "tile", None),
        P(None, None, "tile", None),
        P(("member", "tile")),
        P(("member", "tile")),
        P(("member", "tile")),
        P(("member", "tile")),
        P(),
    )
    out_specs = (P("member", None, "tile", None), P(None, ("member", "tile")))
    return jax.shard_map(
        on_device, mesh=mesh, in_specs=in_specs, out_specs=out_specs, check_vma=False
    )
```

profile of v0, /device:TPU:1, one launch (start us, length us, event | category | flops | bytes accessed | tf_op | source)
XLA Modules:
  0.0 610.6 jit_solution(8120513552935115388)
XLA Ops:
  18.2 4.9 collective-permute-start.3
  25.8 12.7 %copy.124 = f32[10,16,24,128]{1,0,3,2:T(8,128)} copy(f32[10,16,24,128]{3,1,2,0:T(8,128)S(1)} %fusion.10) | data formatting | bytes 3932160 | tf_op jit(solution)/shard_map/reshape | solution.py:56
  38.4 21.0 %reshape.245 = f32[4,1,122880]{2,1,0:T(1,128)} reshape(f32[3072,10,16]{2,1,0:T(8,128)} %bitcast.203) | data formatting | bytes 3932160
  59.5 4.5 all-to-all-start
  66.4 16.0 %all-to-all-done = f32[4,1,122880]{2,1,0:T(1,128)} async-done(((f32[4,1,122880]{2,1,0:T(1,128)}), f32[4,1,122880]{2,1,0:T(1,128)}, u32[]{:S(2)}, u32[]{:S(2)}) %all-to-all-start) | async-done | bytes 1966112 | tf_op jit(solution)/shard_map/all_to_all | solution.py:60
  83.0 7.3 %reduce.29 = f32[4,122880]{1,0:T(4,128)S(1)} reduce(f32[4,1,122880]{2,1,0:T(1,128)} %all-to-all-done, f32[]{:T(128)} %broadcast.321), dimensions={1}, to_apply=%all_to_all.15.reduce_sub_computation | reduce | bytes 3932164 | tf_op jit(solution)/shard_map/all_to_all | solution.py:60
  90.3 17.5 %reshape.246 = f32[3072,10,16]{2,1,0:T(8,128)} reshape(f32[4,122880]{1,0:T(4,128)S(1)} %reduce.29) | data formatting | bytes 3932160
  107.8 15.4 %copy.125 = f32[10,16,4,768]{3,2,1,0:T(4,128)S(1)} copy(f32[10,16,4,768]{1,0,3,2:T(8,128)} %bitcast.202) | data formatting | bytes 3932160 | tf_op jit(solution)/shard_map/all_to_all | solution.py:60
  129.3 4.0 copy.110
  137.6 53.4 %while.13 = (s32[]{:T(128)}, f32[16,40,40]{2,0,1:T(8,128)}, f32[16,40]{1,0:T(8,128)S(1)}, s32[16]{0:T(128)S(1)}, s32[512]{0:T(512)S(1)}, /*index=5*/f32[40,512]{...) while((s32[]{:T(128)}, f32[16,40,40]{2,0,1:T(8,128)}, ...), condition=%wide.region_2.3_spmd, body=%wide.region_1.2_spmd.sunk | while | flops 10118146 | bytes 275805 | solution.py:76
  191.1 85.9 %psum.15 = f32[16,40]{1,0:T(8,128)S(1)} all-reduce(f32[16,40]{1,0:T(8,128)S(1)} %get-tuple-element.46), channel_id=1, replica_groups=mesh['member'=4,'tile'=64] {'member','tile'}, use_global_device_ids=true, to_apply=%region_12.13 | all-reduce | flops 640 | bytes 5120 | tf_op jit(solution)/shard_map/psum | solution.py:77
  277.7 166.3 %all-reduce.5.cloned.1.call-done = f32[16,40,40]{2,0,1:T(8,128)} async-done(((f32[16,40,40]{2,0,1:T(8,128)}), f32[16,40,40]{2,0,1:T(8,128)}) %all-reduce.5.cloned.1.call-update) | async-done | bytes 102416 | tf_op jit(solution)/shard_map/psum | solution.py:77
  443.9 6.1 %convolution_bitcast_fusion = f32[40,12,40,12]{2,1,0,3:T(8,128)} fusion(f32[16,40,40]{2,0,1:T(8,128)} %all-reduce.5.cloned.1.call-done, f32[16,12]{0,1:T(8,128)S(1)} %fusion.68), kind=kOutput, calls=%fused_computation.10 | convolution fusion | flops 44239104 | bytes 1024768 | tf_op jit(solution)/shard_map/lkm,jl,il->kjmi/dot_general | solution.py:78
  450.1 10.4 %copy.126 = f32[40,12,40,12]{1,0,3,2:T(8,128)} copy(f32[40,12,40,12]{2,1,0,3:T(8,128)} %convolution_bitcast_fusion) | data formatting | bytes 1843200 | tf_op jit(solution)/shard_map/reshape | solution.py:78
  460.5 6.6 %reshape.235 = f32[480,480]{0,1:T(8,128)S(1)} reshape(f32[40,12,40,12]{1,0,3,2:T(8,128)} %copy.126) | data formatting | bytes 1843200 | tf_op jit(solution)/shard_map/reshape | solution.py:78
  467.7 11.7 %cholesky.105 = f32[128,128]{1,0:T(8,128)S(1)} custom-call(f32[128,128]{1,0:T(8,128)S(1)} %cholesky.272), custom_call_target="Cholesky" | custom-call | tf_op jit(solution)/shard_map/jit(cholesky)/cholesky | solution.py:83
  479.6 9.8 %custom-call.34 = f32[1,128,128]{1,2,0:T(8,128)S(1)} custom-call(f32[1,128,128]{2,1,0:T(8,128)S(1)} %get-tuple-element.154), custom_call_target="InvertDiagBlocksLowerTriangular" | custom-call | tf_op jit(solution)/shard_map/jit(cholesky)/cholesky | solution.py:83
  490.1 11.7 %cholesky.219 = f32[128,128]{1,0:T(8,128)S(1)} custom-call(f32[128,128]{1,0:T(8,128)S(1)} %cholesky.276), custom_call_target="Cholesky" | custom-call | tf_op jit(solution)/shard_map/jit(cholesky)/cholesky | solution.py:83
  503.2 10.0 %custom-call.35 = f32[1,128,128]{1,2,0:T(8,128)S(1)} custom-call(f32[1,128,128]{2,1,0:T(8,128)S(1)} %get-tuple-element.151), custom_call_target="InvertDiagBlocksLowerTriangular" | custom-call | tf_op jit(solution)/shard_map/jit(cholesky)/cholesky | solution.py:83
  513.8 11.7 %cholesky.240 = f32[128,128]{1,0:T(8,128)S(1)} custom-call(f32[128,128]{1,0:T(8,128)S(1)} %cholesky.281), custom_call_target="Cholesky" | custom-call | tf_op jit(solution)/shard_map/jit(cholesky)/cholesky | solution.py:83
  526.2 9.8 %custom-call.36 = f32[1,128,128]{1,2,0:T(8,128)S(1)} custom-call(f32[1,128,128]{2,1,0:T(8,128)S(1)} %get-tuple-element.148), custom_call_target="InvertDiagBlocksLowerTriangular" | custom-call | tf_op jit(solution)/shard_map/jit(cholesky)/cholesky | solution.py:83
  536.5 8.8 %cholesky.260 = f32[96,96]{1,0:T(8,128)S(1)} custom-call(f32[96,96]{1,0:T(8,128)S(1)} %convolution_subtract_fusion.2), custom_call_target="Cholesky" | custom-call | tf_op jit(solution)/shard_map/jit(cholesky)/cholesky | solution.py:83
  548.6 7.9 %while.14 = (s32[]{:T(128)}, f32[480,480]{1,0:T(8,128)S(1)}, s32[3,2]{0,1:T(2,128)S(1)}, f32[3,128,128]{2,1,0:T(8,128)}, s32[]{:T(128)}) while((s32[]{:T(128)}, f32[480,480]{1,0:T(8,128)S(1)}, s32[3,2]{0,1:T(2,128)S(1)}, f32[3,128,128]{2,1,0:T(8,128)}, s32[]{:T(128)}) %tuple.66), condition=%wide.while_cond, body=%wide.while_body.sunk | while | flops 2 | bytes 132705 | solution.py:84
  557.6 39.6 %custom-call.37 = f32[4,128,128]{1,2,0:T(8,128)S(1)} custom-call(f32[4,128,128]{2,1,0:T(8,128)S(1)} %pad_maximum_fusion.4), custom_call_target="InvertDiagBlocksLowerTriangular" | custom-call | tf_op jit(solution)/shard_map/jit(_cho_solve)/triangular_solve | solution.py:84
  (220 shorter events, 100.7 us)
Async XLA Ops:
  9.1 5.3 collective-permute-start
  11.8 3.9 collective-permute-start.1
  13.2 1.0 copy-start.2
  18.1 5.7 collective-permute-start.2
  18.2 5.8 collective-permute-start.3
  59.5 4.9 copy-start.3
  59.5 4.9 copy-start.6
  59.5 4.9 copy-start.7
  59.5 23.0 %all-to-all-start = ((f32[4,1,122880]{2,1,0:T(1,128)}), f32[4,1,122880]{2,1,0:T(1,128)}, u32[]{:S(2)}, u32[]{:S(2)}) async-start(f32[4,1,122880]{2,1,0:T(1,128)} %reshape.245), calls=%async_computation | async-start | bytes 3932160 | tf_op jit(solution)/shard_map/all_to_all | solution.py:60
  64.0 379.9 %all-reduce.5.cloned.1.call-start = ((), (), s32[]{:S(2)}) async-start(), calls=%async_computation.1 | async-start | bytes 655360 | tf_op jit(solution)/shard_map/psum | solution.py:77
  123.2 1.3 copy-start
  129.3 7.9 %copy-start.5 = (f32[512]{0:T(512)S(1)}, f32[512]{0:T(512)}, u32[]{:S(2)}) copy-start(f32[512]{0:T(512)} %param.14) | copy-start | bytes 6148
  133.3 4.3 copy-start.4
  548.6 51.9 %copy-start.1 = (f32[40,16,768]{2,1,0:T(8,128)S(1)}, f32[40,16,768]{2,1,0:T(8,128)}, u32[]{:S(2)}) copy-start(f32[40,16,768]{2,1,0:T(8,128)} %fusion.26) | copy-start | bytes 5898244
Sparse Core Ops, SparseCore 0:
  191.2 252.6 all-reduce.4
where the time goes:
time: 620 us; the launch traced here: 611 us
  waiting for transfers between devices  184 us (30%)
  local copies, waits for them, and re-layouts  150 us (24%)
  other arithmetic  141 us (23%)
  blocking collectives  85.9 us (14%)
  matrix products  19.2 us (3%)
  between operations  17.5 us (3%)
  starting transfers between devices  13.2 us (2%)
    psum x1, waiting for transfers between devices, on_device(): sums, cross = lax.psum((sums, cross), ('member', 'tile'))  166 us
    psum x1, blocking collectives, on_device(): sums, cross = lax.psum((sums, cross), ('member', 'tile'))  85.9 us
    another operation x15, other arithmetic, on_device(): factor = jnp.linalg.cholesky(system)  76.3 us
    unnamed x21, local copies, waits for them, and re-layouts  44.8 us
    another operation x8, other arithmetic, on_device(): weights = jax.scipy.linalg.cho_solve((factor, True), rhs)  40.8 us
    dynamic_update_slice x32, local copies, waits for them, and re-layouts, on_device(): sums, cross = lax.map(level_terms, jnp.arange(levels))  27.1 us
    all_to_all x3, local copies, waits for them, and re-layouts, on_device(): lax.all_to_all(flat_state, 'member', split_axis=2, concat_axis=0, tiled=T...  17.8 us
    reshape x2, local copies, waits for them, and re-layouts, on_device(): jnp.einsum('lkm,jl,il->kjmi', sums, profiles, profiles, precision=highest)  17 us
  transfers between devices with their start and end apart: 6, of which 4 were waited for; matrix products, arithmetic and copies ran while one was open for 1% of the time, Pallas kernels for 0%

commit v1 on v0

v1 whole, which is shorter than its diff:
```python
import functools
import math

import jax
import jax.numpy as jnp
from jax import lax
from jax.experimental import pallas as pl
from jax.experimental.pallas import tpu as pltpu
from jax.sharding import PartitionSpec as P

MESH = pl.DeviceIdType.MESH
HIGHEST = lax.Precision.HIGHEST
ANY = pl.BlockSpec(memory_space=pl.ANY)
VMEM = pl.BlockSpec(memory_space=pltpu.VMEM)
SMEM = pl.BlockSpec(memory_space=pltpu.SMEM)
N_Y = 4
N_CORE = 2
GROUP = 4
LOCAL = 10
MEMBERS = 40
MODES = 12
LEV = 16
X = 24
CY = 128
RUN = 6
ROWS = LOCAL * LEV
NOBS = 512
TILES = 30
BLOCK = 120
WIDE = 768
VMEM_LIMIT = 48 * 1024 * 1024


def remote(src, dst, send, recv, member, tile):
    return pltpu.make_async_remote_copy(
        src_ref=src,
        dst_ref=dst,
        send_sem=send,
        recv_sem=recv,
        device_id={"member": member, "tile": tile},
        device_id_type=MESH,
    )


def upwind(centre, west, east, cx, cy):
    cx = cx[None]
    cy = cy[None]
    south = pltpu.roll(centre, 1, 2)
    north = pltpu.roll(centre, CY - 1, 2)
    from_x = jnp.where(cx > 0.0, west, east)
    from_y = jnp.where(cy > 0.0, south, north)
    return centre - jnp.abs(cx) * (centre - from_x) - jnp.abs(cy) * (centre - from_y)


def front(
    g1,
    g2,
    piece,
    state_ref,
    courant_ref,
    col_ref,
    lev_ref,
    innov_ref,
    var_ref,
    field_out,
    rows_out,
    sums_ref,
    state,
    courant,
    q0,
    q1,
    q2,
    wind,
    field,
    obs,
    pick,
    held,
    weighted,
    part,
    got,
    red,
    load_sem,
    halo_send,
    halo_recv,
    obs_send,
    obs_recv,
    pick_send,
    pick_recv,
    rs_send,
    rs_recv,
    ex_send,
    ex_recv,
    ag_send,
    ag_recv,
    out_sem,
):
    tiles = lax.axis_size("tile")
    me = lax.axis_index("member")
    tile = lax.axis_index("tile")
    core = lax.rem(tile, N_CORE)
    y = lax.rem(tile // N_CORE, N_Y)
    z = tile // (N_CORE * N_Y)
    right = lax.rem(tile + 1, tiles)
    left = lax.rem(tile + tiles - 1, tiles)
    a = me * N_Y + y
    b = z * N_CORE + core

    def peer_a(r):
        other = lax.rem(a + r, g1)
        return other, other // N_Y, (z * N_Y + lax.rem(other, N_Y)) * N_CORE + core

    def peer_b(r):
        other = lax.rem(b + r, g2)
        return other, me, ((other // N_CORE) * N_Y + y) * N_CORE + lax.rem(other, N_CORE)

    loads = [
        pltpu.make_async_copy(state_ref, state, load_sem.at[0]),
        pltpu.make_async_copy(courant_ref, courant, load_sem.at[1]),
    ]
    for copy in loads:
        copy.start()

    barrier = pltpu.get_barrier_semaphore()
    for other in (left, right):
        pl.semaphore_signal(barrier, 1, device_id={"member": me, "tile": other}, device_id_type=MESH)

    def greet_a(r, _):
        _, m, t = peer_a(r)
        pl.semaphore_signal(barrier, 1, device_id={"member": m, "tile": t}, device_id_type=MESH)
        return 0

    def greet_b(r, _):
        _, m, t = peer_b(r)
        pl.semaphore_signal(barrier, 1, device_id={"member": m, "tile": t}, device_id_type=MESH)
        return 0

    lax.fori_loop(1, g1, greet_a, 0)
    lax.fori_loop(1, g2, greet_b, 0)

    obs[me] = jnp.broadcast_to(lev_ref[...] * 1024 + col_ref[...], (8, NOBS))
    for copy in loads:
        copy.wait()

    def turn(x, _):
        q0[x + 2] = state[pl.ds(x, ROWS, stride=X), :]
        wind[x + 1] = courant[pl.ds(x, 2 * LEV, stride=X), :]
        return 0

    for x in (0, 1, 22, 23):
        turn(x, 0)

    pl.semaphore_wait(barrier, 2 + (g1 - 1) + (g2 - 1))

    halos = [
        remote(q0.at[pl.ds(X, 2)], q0.at[pl.ds(0, 2)], halo_send.at[0], halo_recv.at[0], me, right),
        remote(wind.at[X], wind.at[0], halo_send.at[1], halo_recv.at[1], me, right),
        remote(q0.at[pl.ds(2, 2)], q0.at[pl.ds(X + 2, 2)], halo_send.at[2], halo_recv.at[2], me, left),
        remote(wind.at[1], wind.at[X + 1], halo_send.at[3], halo_recv.at[3], me, left),
    ]
    for copy in halos:
        copy.start()
    obs_copies = []
    for r in range(1, GROUP):
        to = lax.rem(me + r, GROUP)
        copy = remote(obs.at[me], obs.at[me], obs_send.at[r - 1], obs_recv.at[r - 1], to, tile)
        copy.start()
        obs_copies.append(copy)

    lax.fori_loop(2, 22, turn, 0)

    def first(i, _):
        w = wind[i]
        new = upwind(
            q0[i + 1].reshape(LOCAL, LEV, CY),
            q0[i].reshape(LOCAL, LEV, CY),
            q0[i + 2].reshape(LOCAL, LEV, CY),
            w[:LEV],
            w[LEV:],
        )
        q1[i] = new.reshape(ROWS, CY)
        return 0

    def second(i, _):
        w = wind[i + 1]
        new = upwind(
            q1[i + 1].reshape(LOCAL, LEV, CY),
            q1[i].reshape(LOCAL, LEV, CY),
            q1[i + 2].reshape(LOCAL, LEV, CY),
            w[:LEV],
            w[LEV:],
        ).reshape(ROWS, CY)
        q2[i] = new
        field[pl.ds(i, ROWS, stride=X), :] = new
        return 0

    lax.fori_loop(2, X, first, 0)
    for copy in halos:
        copy.wait_recv()
    for i in (0, 1, X, X + 1):
        first(i, 0)
    lax.fori_loop(0, X, second, 0)

    outs = [
        pltpu.make_async_copy(field, field_out, out_sem.at[0]),
        pltpu.make_async_copy(q2, rows_out, out_sem.at[1]),
    ]
    for copy in outs:
        copy.start()

    for copy in obs_copies:
        copy.wait_recv()

    sub_y = lax.broadcasted_iota(jnp.int32, (CY, NOBS), 0)
    sub_l = lax.broadcasted_iota(jnp.int32, (LEV, NOBS), 0)

    def pick_for(owner):
        code = obs[owner][:1]
        spot = code & 1023
        row = lax.shift_right_logical(code, 10) * 8 + lax.shift_right_logical(spot, 7)
        hot = (sub_y == (spot & 127)).astype(jnp.bfloat16)
        total = jnp.zeros((LOCAL, LEV, NOBS), jnp.float32)
        for x in range(RUN):
            cells = q2[owner * RUN + x]
            high = cells.astype(jnp.bfloat16)
            rest = cells - high.astype(jnp.float32)
            mid = rest.astype(jnp.bfloat16)
            low = (rest - mid.astype(jnp.float32)).astype(jnp.bfloat16)
            found = sum(jnp.dot(p, hot, preferred_element_type=jnp.float32) for p in (high, mid, low))
            here = (row == sub_l * 8 + x)[None]
            total = total + jnp.where(here, found.reshape(LOCAL, LEV, NOBS), 0.0)
        return jnp.sum(total, axis=1)

    pick_copies = []
    for r in range(1, GROUP):
        to = lax.rem(me + r, GROUP)
        pick[r - 1, :LOCAL] = pick_for(to)
        pick[r - 1, LOCAL:] = jnp.zeros((16 - LOCAL, NOBS), jnp.float32)
        copy = remote(pick.at[r - 1], held.at[me], pick_send.at[r - 1], pick_recv.at[r - 1], to, tile)
        copy.start()
        pick_copies.append(copy)
    held[me, :LOCAL] = pick_for(me)
    for copy in pick_copies:
        copy.wait_recv()

    picked = jnp.concatenate([held[m][:LOCAL] for m in range(GROUP)], axis=0)
    mean = jnp.sum(picked, axis=0, keepdims=True) * (1.0 / MEMBERS)
    anomaly = (picked - mean) * (1.0 / math.sqrt(MEMBERS - 1.0))
    inverse = 1.0 / var_ref[...]
    scaled = anomaly * inverse
    innov = innov_ref[...] * inverse
    level = lev_ref[...]
    for l in range(LEV):
        weighted[l * MEMBERS : (l + 1) * MEMBERS] = jnp.where(level == l, scaled, 0.0)
    own_level = lax.broadcasted_iota(jnp.int32, (LEV, NOBS), 0) == level
    weighted[LEV * MEMBERS : LEV * MEMBERS + LEV] = jnp.where(own_level, innov, 0.0)
    weighted[LEV * MEMBERS + LEV :] = jnp.zeros((WIDE - LEV * MEMBERS - LEV, NOBS), jnp.float32)
    sums = lax.dot_general(
        anomaly,
        weighted[...],
        (((1,), (1,)), ((), ())),
        precision=HIGHEST,
        preferred_element_type=jnp.float32,
    )
    for q in range(TILES):
        s, c = q // 6, q % 6
        part[q // piece, (q % piece) * 8 : (q % piece) * 8 + 8] = sums[s * 8 : s * 8 + 8, c * 128 : c * 128 + 128]
    for q in range(TILES, g1 * piece):
        part[q // piece, (q % piece) * 8 : (q % piece) * 8 + 8] = jnp.zeros((8, 128), jnp.float32)

    def rs_copy(r):
        other, m, t = peer_a(r)
        return remote(part.at[other], got.at[r - 1], rs_send.at[r - 1], rs_recv.at[r - 1], m, t)

    def ex_copy(r):
        other, m, t = peer_b(r)
        return remote(red.at[b], red.at[b], ex_send.at[r - 1], ex_recv.at[r - 1], m, t)

    def ag_copy(r):
        other, m, t = peer_a(r)
        return remote(sums_ref.at[a], sums_ref.at[a], ag_send.at[r - 1], ag_recv.at[r - 1], m, t)

    for r in range(1, g1):
        rs_copy(r).start()
    for r in range(1, g1):
        rs_copy(r).wait_recv()
    red[b] = part[a] + jnp.sum(got[...], axis=0)
    for r in range(1, g2):
        ex_copy(r).start()
    for r in range(1, g2):
        ex_copy(r).wait_recv()
    sums_ref[a] = jnp.sum(red[...], axis=0)
    for r in range(1, g1):
        ag_copy(r).start()
    for r in range(1, g1):
        ag_copy(r).wait_recv()

    for copy in halos + obs_copies + pick_copies:
        copy.wait_send()
    for r in range(1, g1):
        rs_copy(r).wait_send()
        ag_copy(r).wait_send()
    for r in range(1, g2):
        ex_copy(r).wait_send()
    for copy in outs:
        copy.wait()


def inverse_of(tiles):
    lane = lax.broadcasted_iota(jnp.int32, (8, 128), 1)
    sub = lax.broadcasted_iota(jnp.int32, (8, 128), 0)
    count = len(tiles)
    tiles = list(tiles)
    for p in range(count):
        rows = tiles[p]
        for j in range(8):
            c = 8 * p + j
            column = jnp.broadcast_to(rows[:, c : c + 1], (8, 128))
            pivot = jnp.broadcast_to(column[j : j + 1], (8, 128))
            line = jnp.broadcast_to(rows[j : j + 1], (8, 128))
            line = jnp.where(lane == c, 1.0, line) / pivot
            base = jnp.where((lane == c) | (sub == j), 0.0, rows)
            rows = base - jnp.where(sub == j, -1.0, column) * line
        tiles[p] = rows
        inside = (lane >= 8 * p) & (lane < 8 * p + 8)
        lines = [jnp.broadcast_to(rows[j : j + 1], (8, 128)) for j in range(8)]
        for t in range(count):
            if t == p:
                continue
            old = tiles[t]
            new = jnp.where(inside, 0.0, old)
            for j in range(8):
                c = 8 * p + j
                new = new - jnp.broadcast_to(old[:, c : c + 1], (8, 128)) * lines[j]
            tiles[t] = new
    return tiles


def dot(left, right):
    return jnp.dot(left, right, precision=HIGHEST, preferred_element_type=jnp.float32)


def solve(piece, sums_ref, waves_ref, field_ref, coeff_ref, advanced_ref, gram, left, right, system, block, line, copy_sem):
    keep = pltpu.make_async_copy(field_ref, advanced_ref, copy_sem)
    keep.start()
    for q in range(TILES):
        s, c = q // 6, q % 6
        gram[s * 8 : s * 8 + 8, c * 128 : c * 128 + 128] = sums_ref[q // piece, (q % piece) * 8 : (q % piece) * 8 + 8]

    def cosines(wave, level):
        return jnp.cos(jnp.pi * wave * (level.astype(jnp.float32) + 0.5) / LEV)

    def by_mode(mode):
        wave = jnp.zeros(mode.shape, jnp.float32)
        scale = jnp.zeros(mode.shape, jnp.float32)
        for j in range(MODES):
            wave = jnp.where(mode == j, waves_ref[j].astype(jnp.float32), wave)
            scale = jnp.where(mode == j, 1.0 / math.sqrt(1.0 + j), scale)
        return wave, scale

    def iota(shape, axis):
        return lax.broadcasted_iota(jnp.int32, shape, axis)

    lane = iota((16, WIDE), 1)
    level = jnp.where(lane < LEV * MEMBERS, lane // MEMBERS, lane - LEV * MEMBERS)
    wave, scale = by_mode(iota((16, WIDE), 0))
    line[...] = jnp.where(lane < LEV * MEMBERS + LEV, scale * cosines(wave, level), 0.0)
    for i in range(MODES):
        left[i * MEMBERS : (i + 1) * MEMBERS] = gram[...] * line[i : i + 1]
    lane = iota((16, 512), 1)
    inner = lane % 128
    mode = jnp.where(inner < BLOCK, (lane // 128) * 3 + inner // MEMBERS, MODES)
    wave, scale = by_mode(mode)
    table = scale * cosines(wave, iota((16, 512), 0))
    lane = iota((MEMBERS, 512), 1)
    same = ((lane % 128) % MEMBERS) == iota((MEMBERS, 512), 0)
    for l in range(LEV):
        right[l * MEMBERS : (l + 1) * MEMBERS] = jnp.where(same, table[l : l + 1], 0.0)
    spot = 3 * 128 + BLOCK
    tail = WIDE - LEV * MEMBERS
    at = (iota((tail, 512), 1) == spot) & (iota((tail, 512), 0) < LEV)
    right[LEV * MEMBERS :] = jnp.where(at, 1.0, 0.0)
    system[...] = dot(left[...], right[...])

    diag = (iota((BLOCK, 128), 0) == iota((BLOCK, 128), 1)).astype(jnp.float32)
    for p in range(4):
        here = slice(p * BLOCK, (p + 1) * BLOCK)
        cols = slice(p * 128, (p + 1) * 128)
        own = system[here, cols] + diag
        own = jnp.where(iota((BLOCK, 128), 1) < BLOCK, own, 0.0)
        done = inverse_of([own[8 * t : 8 * t + 8] for t in range(BLOCK // 8)])
        for t in range(BLOCK // 8):
            block[8 * t : 8 * t + 8] = done[t]
        rest = slice(min((p + 1) * 128, 384), 512)
        new = dot(block[...][:, :BLOCK], system[here, rest])
        for q in range(4):
            if q != p:
                there = slice(q * BLOCK, (q + 1) * BLOCK)
                system[there, rest] = system[there, rest] - dot(system[there, cols][:, :BLOCK], new)
        system[here, rest] = new

    lane = iota((16, 128), 1)
    wave, scale = by_mode(iota((16, 128), 0))
    table = jnp.where(lane < LEV, scale * cosines(wave, lane), 0.0)
    total = jnp.zeros((MEMBERS, 128), jnp.float32)
    for j in range(MODES):
        weight = system[j * MEMBERS : (j + 1) * MEMBERS, 384:512][:, BLOCK : BLOCK + 1]
        total = total + weight * table[j : j + 1]
    mean = jnp.sum(total, axis=0, keepdims=True) * (1.0 / MEMBERS)
    total = (total - mean) * (1.0 / math.sqrt(MEMBERS - 1.0))
    turned = jnp.concatenate([total, jnp.zeros((128 - MEMBERS, 128), jnp.float32)], axis=0).T[:LEV]
    for k in range(MEMBERS):
        coeff_ref[k] = jnp.broadcast_to(turned[:, k : k + 1], (LEV, 128))
    keep.wait()


def finish(coeff_ref, rows_ref, out_ref, part, got, send_sem, recv_sem):
    me = lax.axis_index("member")
    tile = lax.axis_index("tile")
    barrier = pltpu.get_barrier_semaphore()
    for r in range(1, GROUP):
        to = lax.rem(me + r, GROUP)
        pl.semaphore_signal(barrier, 1, device_id={"member": to, "tile": tile}, device_id_type=MESH)

    def run_for(owner, slot):
        for x in range(RUN):
            total = jnp.zeros((LEV, CY), jnp.float32)
            for k in range(LOCAL):
                total = total + rows_ref[owner * RUN + x, k * LEV : (k + 1) * LEV] * coeff_ref[me * LOCAL + k]
            part[slot, x] = total

    copies = []
    for r in range(1, GROUP):
        to = lax.rem(me + r, GROUP)
        run_for(to, r)
        if r == 1:
            pl.semaphore_wait(barrier, GROUP - 1)
        copy = remote(part.at[r], got.at[r - 1], send_sem.at[r - 1], recv_sem.at[r - 1], to, tile)
        copy.start()
        copies.append(copy)
    run_for(me, 0)
    for copy in copies:
        copy.wait_recv()
    for x in range(RUN):
        out_ref[:, x * CY : (x + 1) * CY] = part[0, x] + got[0, x] + got[1, x] + got[2, x]
    for copy in copies:
        copy.wait_send()


def on_device(member_state, courant, obs_col, obs_lev, innovation, obs_var, mode_waves):
    tiles = lax.axis_size("tile")
    g1 = GROUP * N_Y
    g2 = tiles // N_Y
    piece = -(-TILES // g1)
    f32 = jnp.float32
    dma = pltpu.SemaphoreType.DMA
    shape = member_state.shape
    field, rows, sums = pl.pallas_call(
        functools.partial(front, g1, g2, piece),
        out_shape=[
            jax.ShapeDtypeStruct((ROWS * X, CY), f32),
            jax.ShapeDtypeStruct((X, ROWS, CY), f32),
            jax.ShapeDtypeStruct((g1, piece * 8, 128), f32),
        ],
        in_specs=[ANY, ANY, VMEM, VMEM, VMEM, VMEM],
        out_specs=[ANY, ANY, VMEM],
        scratch_shapes=[
            pltpu.VMEM((ROWS * X, CY), f32),
            pltpu.VMEM((2 * LEV * X, CY), f32),
            pltpu.VMEM((X + 4, ROWS, CY), f32),
            pltpu.VMEM((X + 2, ROWS, CY), f32),
            pltpu.VMEM((X, ROWS, CY), f32),
            pltpu.VMEM((X + 2, 2 * LEV, CY), f32),
            pltpu.VMEM((ROWS * X, CY), f32),
            pltpu.VMEM((GROUP, 8, NOBS), jnp.int32),
            pltpu.VMEM((GROUP - 1, 16, NOBS), f32),
            pltpu.VMEM((GROUP, 16, NOBS), f32),
            pltpu.VMEM((WIDE, NOBS), f32),
            pltpu.VMEM((g1, piece * 8, 128), f32),
            pltpu.VMEM((g1 - 1, piece * 8, 128), f32),
            pltpu.VMEM((g2, piece * 8, 128), f32),
            dma((2,)),
            dma((4,)),
            dma((4,)),
            dma((GROUP - 1,)),
            dma((GROUP - 1,)),
            dma((GROUP - 1,)),
            dma((GROUP - 1,)),
            dma((g1 - 1,)),
            dma((g1 - 1,)),
            dma((g2 - 1,)),
            dma((g2 - 1,)),
            dma((g1 - 1,)),
            dma((g1 - 1,)),
            dma((2,)),
        ],
        compiler_params=pltpu.CompilerParams(
            collective_id=0, has_side_effects=True, vmem_limit_bytes=VMEM_LIMIT
        ),
        name="front",
    )(
        member_state.reshape(ROWS * X, CY),
        courant.reshape(2 * LEV * X, CY),
        obs_col.reshape(1, NOBS),
        obs_lev.reshape(1, NOBS),
        innovation.reshape(1, NOBS),
        obs_var.reshape(1, NOBS),
    )
    coeffs, advanced = pl.pallas_call(
        functools.partial(solve, piece),
        out_shape=[
            jax.ShapeDtypeStruct((MEMBERS, LEV, 128), f32),
            jax.ShapeDtypeStruct((ROWS * X, CY), f32),
        ],
        in_specs=[VMEM, SMEM, ANY],
        out_specs=[VMEM, ANY],
        scratch_shapes=[
            pltpu.VMEM((MEMBERS, WIDE), f32),
            pltpu.VMEM((MODES * MEMBERS, WIDE), f32),
            pltpu.VMEM((WIDE, 512), f32),
            pltpu.VMEM((MODES * MEMBERS, 512), f32),
            pltpu.VMEM((BLOCK, 128), f32),
            pltpu.VMEM((16, WIDE), f32),
            dma,
        ],
        compiler_params=pltpu.CompilerParams(vmem_limit_bytes=VMEM_LIMIT),
        name="solve",
    )(sums, mode_waves, field)
    increment = pl.pallas_call(
        finish,
        out_shape=jax.ShapeDtypeStruct((LEV, RUN * CY), f32),
        in_specs=[VMEM, VMEM],
        out_specs=VMEM,
        scratch_shapes=[
            pltpu.VMEM((GROUP, RUN, LEV, CY), f32),
            pltpu.VMEM((GROUP - 1, RUN, LEV, CY), f32),
            dma((GROUP - 1,)),
            dma((GROUP - 1,)),
        ],
        compiler_params=pltpu.CompilerParams(
            collective_id=1, has_side_effects=True, vmem_limit_bytes=VMEM_LIMIT
        ),
        name="finish",
    )(coeffs, rows)
    return advanced.reshape(shape), increment


def solution(mesh):
    in_specs = (
        P("member", None, "tile", None),
        P(None, None, "tile", None),
        P(("member", "tile")),
        P(("member", "tile")),
        P(("member", "tile")),
        P(("member", "tile")),
        P(),
    )
    out_specs = (P("member", None, "tile", None), P(None, ("member", "tile")))
    return jax.shard_map(
        on_device, mesh=mesh, in_specs=in_specs, out_specs=out_specs, check_vma=False
    )
```

time: 620 us -> 127 us (0.20); the launches traced: 611 us -> 126 us
  waiting for transfers between devices: 184 us -> 0 us
  local copies, waits for them, and re-layouts: 150 us -> 4.35 us
  other arithmetic: 141 us -> 0 us
  Pallas kernels: 0 us -> 121 us
  blocking collectives: 85.9 us -> 0 us
  matrix products: 19.2 us -> 0 us
  between operations: 17.5 us -> 0.68 us
  starting transfers between devices: 13.2 us -> 0 us
    psum x1 -> x0, waiting for transfers between devices: 166 us -> none  [on_device(): sums, cross = lax.psum((sums, cross), ('member', 'tile'))]
    pallas_call x0 -> x3, Pallas kernels: none -> 121 us  [the longest x1 72.4 us: on_device(): pl.pallas_call(functools.partial(solve, piece), out_shape=[jax.ShapeDtype...]
    another operation x23 -> x0, other arithmetic: 117 us -> none  [the longest x15 76.3 us: on_device(): factor = jnp.linalg.cholesky(system)]
    psum x1 -> x0, blocking collectives: 85.9 us -> none  [on_device(): sums, cross = lax.psum((sums, cross), ('member', 'tile'))]
    unnamed x21 -> x13, local copies, waits for them, and re-layouts: 44.8 us -> 4.35 us
    reshape x4 -> x0, local copies, waits for them, and re-layouts: 29.8 us -> none  [the longest x2 17 us: on_device(): jnp.einsum('lkm,jl,il->kjmi', sums, profiles, profiles, precision=highest)]
    dynamic_update_slice x32 -> x0, local copies, waits for them, and re-layouts: 27.1 us -> none  [on_device(): sums, cross = lax.map(level_terms, jnp.arange(levels))]
    all_to_all x3 -> x0, local copies, waits for them, and re-layouts: 17.8 us -> none  [on_device(): lax.all_to_all(flat_state, 'member', split_axis=2, concat_axis=0, tiled=T...]
  transfers between devices with their start and end apart: 6 -> 0, of which waited for: 4 -> 0; matrix products, arithmetic and copies ran while one was open for 1% -> 0% of each run, Pallas kernels for 0% -> 0%
where the time goes in v1:
time: 127 us; the launch traced here: 126 us
  Pallas kernels  121 us (95%)
  local copies, waits for them, and re-layouts  4.35 us (3%)
    pallas_call x1, Pallas kernels, on_device(): pl.pallas_call(functools.partial(solve, piece), out_shape=[jax.ShapeDtype...  72.4 us
    pallas_call x1, Pallas kernels, on_device(): pl.pallas_call(functools.partial(front, g1, g2, piece), out_shape=[jax.Sh...  43.6 us
    pallas_call x1, Pallas kernels, on_device(): pl.pallas_call(finish, out_shape=jax.ShapeDtypeStruct((LEV, RUN * CY), f3...  5.21 us
    unnamed x13, local copies, waits for them, and re-layouts  4.35 us

profile of v1, /device:TPU:1, one launch (start us, length us, event | category | flops | bytes accessed | tf_op | source)
XLA Modules:
  0.0 126.3 jit_solution(9797231305650454538)
XLA Ops:
  0.6 0.0 copy-start.5
  0.6 0.0 copy-start
  0.7 1.0 copy-done
  1.6 0.0 copy-start.1
  1.6 0.7 copy-done.1
  2.3 0.0 copy-start.2
  2.3 0.7 copy-done.2
  3.0 0.0 copy-start.3
  3.0 0.7 copy-done.3
  3.7 0.0 copy-start.4
  3.7 0.7 copy-done.4
  4.4 43.6 %front.1 = (f32[3840,128]{1,0:T(8,128)S(1)}, f32[24,160,128]{2,1,0:T(8,128)S(1)}, f32[16,16,128]{2,1,0:T(8,128)S(1)}) custom-call(f32[3840,128]{1,0:T(8,128)} %bitcast.12, f32[768,128]{1,0:T(8,128)S(1)} %bitcast.7, s32[1,512]{1,0:T(1,128)S(1)} %bitcast.8, s32[1,512]{1,0:T(1,128)S(1)} %bitcast.9, f32[1,512]{1,0:T(1,128)S(1)} %bitcast.10, f32[1,512]{1,0:T(1,128)S(1)} %bitcast.11), custom_call_target="tpu_custom_call" | custom-call | tf_op jit(solution)/shard_map/front/pallas_call | solution.py:457
  48.0 0.0 copy-done.5
  48.0 72.4 %solve.1 = (f32[40,16,128]{2,1,0:T(8,128)S(1)}, f32[3840,128]{1,0:T(8,128)}) custom-call(f32[16,16,128]{2,1,0:T(8,128)S(1)} %get-tuple-element.7.sums_ref, s32[12]{0:T(128)S(1)} %copy-done.5, f32[3840,128]{1,0:T(8,128)S(1)} %get-tuple-element.8.field_ref), custom_call_target="tpu_custom_call" | custom-call | tf_op jit(solution)/shard_map/solve/pallas_call | solution.py:508
  120.4 5.2 %finish.1 = f32[16,768]{1,0:T(8,128)S(1)} custom-call(f32[40,16,128]{2,1,0:T(8,128)S(1)} %get-tuple-element.10.coeff_ref, f32[24,160,128]{2,1,0:T(8,128)S(1)} %get-tuple-element.11.rows_ref), custom_call_target="tpu_custom_call" | custom-call | tf_op jit(solution)/shard_map/finish/pallas_call | solution.py:528
  125.6 0.6 copy.10
Async XLA Ops:
  0.6 47.4 %copy-start.5 = (s32[12]{0:T(128)S(1)}, s32[12]{0:T(128)}, u32[]{:S(2)}) copy-start(s32[12]{0:T(128)} %waves_ref.1) | copy-start | bytes 148
  0.6 1.0 copy-start
  1.6 0.7 copy-start.1
  2.3 0.7 copy-start.2
  3.0 0.7 copy-start.3
  3.7 0.7 copy-start.4

commit v2 on v1

v2 whole, which is shorter than its diff:
```python
import functools
import math

import jax
import jax.numpy as jnp
from jax import lax
from jax.experimental import pallas as pl
from jax.experimental.pallas import tpu as pltpu
from jax.sharding import PartitionSpec as P

MESH = pl.DeviceIdType.MESH
HIGHEST = lax.Precision.HIGHEST
ANY = pl.BlockSpec(memory_space=pl.ANY)
VMEM = pl.BlockSpec(memory_space=pltpu.VMEM)
SMEM = pl.BlockSpec(memory_space=pltpu.SMEM)
N_Y = 4
N_CORE = 2
GROUP = 4
LOCAL = 10
MEMBERS = 40
MODES = 12
LEV = 16
X = 24
CY = 128
RUN = 6
ROWS = LOCAL * LEV
NOBS = 512
TILES = 30
BLOCK = 120
WIDE = 768
VMEM_LIMIT = 56 * 1024 * 1024


def remote(src, dst, send, recv, member, tile):
    return pltpu.make_async_remote_copy(
        src_ref=src,
        dst_ref=dst,
        send_sem=send,
        recv_sem=recv,
        device_id={"member": member, "tile": tile},
        device_id_type=MESH,
    )


def upwind(centre, west, east, wind):
    cx = wind[:LEV][None]
    cy = wind[LEV:][None]
    lane = lax.broadcasted_iota(jnp.int32, (1, LEV, CY), 2)
    source = jnp.broadcast_to((lane + jnp.where(cy > 0.0, -1, 1)) & (CY - 1), (LOCAL, LEV, CY))
    from_y = jnp.take_along_axis(centre, source.reshape(ROWS, CY), axis=1)
    centre, west, east, from_y = (v.reshape(LOCAL, LEV, CY) for v in (centre, west, east, from_y))
    from_x = jnp.where(cx > 0.0, west, east)
    new = centre - jnp.abs(cx) * (centre - from_x) - jnp.abs(cy) * (centre - from_y)
    return new.reshape(ROWS, CY)


def offset(group, r):
    member = shift = 0
    for bits, place in reversed(group):
        part = r & ((1 << bits) - 1)
        r >>= bits
        if place is None:
            member = part
        else:
            shift |= part << place
    return member, shift


def far_first(group):
    def hops(r):
        total = 0.0
        for bits, place in reversed(group):
            part = r & ((1 << bits) - 1)
            r >>= bits
            if place != 0:
                total += (0.0, 1.0, 2.0, 1.0)[part] if bits == 2 else (0.0, 1.0, 2.0, 2.2, 4.0, 3.0, 2.4, 1.5)[part]
        return total

    count = 1 << sum(bits for bits, _ in group)
    return sorted(range(1, count), key=lambda r: -hops(r))


def front(
    plane,
    depth,
    piece,
    state_ref,
    courant_ref,
    col_in,
    lev_in,
    innov_in,
    var_in,
    field_out,
    rows_out,
    sums_ref,
    state,
    courant,
    q0,
    q1,
    q2,
    wind,
    field,
    col_ref,
    lev_ref,
    innov_ref,
    var_ref,
    obs,
    pick,
    held,
    weighted,
    part,
    got,
    red,
    mine,
    more,
    last,
    load_sem,
    halo_send,
    halo_recv,
    obs_send,
    obs_recv,
    pick_send,
    pick_recv,
    rs_send,
    rs_recv,
    ex_send,
    ex_recv,
    ag_send,
    ag_recv,
    out_sem,
):
    tiles = lax.axis_size("tile")
    me = lax.axis_index("member")
    tile = lax.axis_index("tile")
    right = lax.rem(tile + 1, tiles)
    left = lax.rem(tile + tiles - 1, tiles)
    plane_order, depth_order = far_first(plane), far_first(depth)
    a = me * N_Y + (lax.shift_right_logical(tile, 1) & (N_Y - 1))

    def peer(group, r):
        member, shift = offset(group, r)
        return me ^ member, tile ^ shift

    loads = [
        pltpu.make_async_copy(state_ref, state, load_sem.at[0]),
        pltpu.make_async_copy(courant_ref, courant, load_sem.at[1]),
        pltpu.make_async_copy(col_in, col_ref, load_sem.at[2]),
        pltpu.make_async_copy(lev_in, lev_ref, load_sem.at[3]),
        pltpu.make_async_copy(innov_in, innov_ref, load_sem.at[4]),
        pltpu.make_async_copy(var_in, var_ref, load_sem.at[5]),
    ]
    for copy in loads:
        copy.start()

    barrier = pltpu.get_barrier_semaphore()

    def greet(m, t):
        pl.semaphore_signal(barrier, 1, device_id={"member": m, "tile": t}, device_id_type=MESH)

    for other in (left, right):
        greet(me, other)
    for r in depth_order:
        greet(*peer(depth, r))
    for r in plane_order:
        greet(*peer(plane, r))

    for copy in loads[2:]:
        copy.wait()
    obs[me] = jnp.broadcast_to(lev_ref[...] * 1024 + col_ref[...], (8, NOBS))
    for copy in loads[:2]:
        copy.wait()

    def turn(x, _):
        q0[x + 2] = state[pl.ds(x, ROWS, stride=X), :]
        wind[x + 1] = courant[pl.ds(x, 2 * LEV, stride=X), :]
        return 0

    for x in (0, 1, 22, 23):
        turn(x, 0)

    pl.semaphore_wait(barrier, 2 + len(plane_order) + len(depth_order))

    halos = [
        remote(q0.at[pl.ds(X, 2)], q0.at[pl.ds(0, 2)], halo_send.at[0], halo_recv.at[0], me, right),
        remote(wind.at[X], wind.at[0], halo_send.at[1], halo_recv.at[1], me, right),
        remote(q0.at[pl.ds(2, 2)], q0.at[pl.ds(X + 2, 2)], halo_send.at[2], halo_recv.at[2], me, left),
        remote(wind.at[1], wind.at[X + 1], halo_send.at[3], halo_recv.at[3], me, left),
    ]
    for copy in halos:
        copy.start()
    obs_copies = []
    for r in (2, 1, 3):
        to = me ^ r
        copy = remote(obs.at[me], obs.at[me], obs_send.at[r - 1], obs_recv.at[r - 1], to, tile)
        copy.start()
        obs_copies.append(copy)

    lax.fori_loop(2, 22, turn, 0)

    def first(i, _):
        q1[i] = upwind(q0[i + 1], q0[i], q0[i + 2], wind[i])
        return 0

    def second(i, _):
        q2[i] = upwind(q1[i + 1], q1[i], q1[i + 2], wind[i + 1])
        return 0

    def pack(i, _):
        field[pl.ds(i, ROWS, stride=X), :] = q2[i]
        return 0

    lax.fori_loop(2, X, first, 0, unroll=2)
    for copy in halos:
        copy.wait_recv()
    for i in (0, 1, X, X + 1):
        first(i, 0)
    lax.fori_loop(0, X, second, 0, unroll=4)

    outs = [pltpu.make_async_copy(q2, rows_out, out_sem.at[1])]
    outs[0].start()

    for copy in obs_copies:
        copy.wait_recv()

    sub_y = lax.broadcasted_iota(jnp.int32, (CY, NOBS), 0)
    sub_l = lax.broadcasted_iota(jnp.int32, (LEV, NOBS), 0)

    def pick_for(owner):
        code = obs[owner][:1]
        spot = code & 1023
        row = lax.shift_right_logical(code, 10) * 8 + lax.shift_right_logical(spot, 7)
        hot = (sub_y == (spot & 127)).astype(jnp.bfloat16)
        twice = jnp.concatenate([hot, hot], axis=0)
        total = jnp.zeros((LOCAL, LEV, NOBS), jnp.float32)
        for x in range(RUN):
            cells = q2[owner * RUN + x]
            high = cells.astype(jnp.bfloat16)
            rest = cells - high.astype(jnp.float32)
            mid = rest.astype(jnp.bfloat16)
            low = (rest - mid.astype(jnp.float32)).astype(jnp.bfloat16)
            found = jnp.dot(
                jnp.concatenate([high, mid], axis=1), twice, preferred_element_type=jnp.float32
            ) + jnp.dot(low, hot, preferred_element_type=jnp.float32)
            here = (row == sub_l * 8 + x)[None]
            total = total + jnp.where(here, found.reshape(LOCAL, LEV, NOBS), 0.0)
        return jnp.sum(total, axis=1)

    pick_copies = []
    for r in (2, 1, 3):
        to = me ^ r
        pick[r - 1, :LOCAL] = pick_for(to)
        pick[r - 1, LOCAL:] = jnp.zeros((16 - LOCAL, NOBS), jnp.float32)
        copy = remote(pick.at[r - 1], held.at[me], pick_send.at[r - 1], pick_recv.at[r - 1], to, tile)
        copy.start()
        pick_copies.append(copy)
    held[me, :LOCAL] = pick_for(me)
    lax.fori_loop(0, X, pack, 0, unroll=4)
    outs.append(pltpu.make_async_copy(field, field_out, out_sem.at[0]))
    outs[1].start()
    for copy in pick_copies:
        copy.wait_recv()

    picked = jnp.concatenate([held[m][:LOCAL] for m in range(GROUP)], axis=0)
    mean = jnp.sum(picked, axis=0, keepdims=True) * (1.0 / MEMBERS)
    anomaly = (picked - mean) * (1.0 / math.sqrt(MEMBERS - 1.0))
    inverse = 1.0 / var_ref[...]
    scaled = anomaly * inverse
    innov = innov_ref[...] * inverse
    level = lev_ref[...]
    for l in range(LEV):
        at = (l // 3) * 128 + (l % 3) * MEMBERS
        weighted[at : at + MEMBERS] = jnp.where(level == l, scaled, 0.0)
    sub = lax.broadcasted_iota(jnp.int32, (8, NOBS), 0)
    for t in range(6):
        held_here = (level == sub + 3 * t) & (sub < 3)
        weighted[t * 128 + BLOCK : t * 128 + 128] = jnp.where(held_here, innov, 0.0)
    weighted[5 * 128 + MEMBERS : 5 * 128 + BLOCK] = jnp.zeros((BLOCK - MEMBERS, NOBS), jnp.float32)
    sums = lax.dot_general(
        anomaly,
        weighted[...],
        (((1,), (1,)), ((), ())),
        precision=HIGHEST,
        preferred_element_type=jnp.float32,
    )
    for q in range(TILES):
        s, c = q // 6, q % 6
        part[q // piece, (q % piece) * 8 : (q % piece) * 8 + 8] = sums[s * 8 : s * 8 + 8, c * 128 : c * 128 + 128]
    for q in range(TILES, part.shape[0] * piece):
        part[q // piece, (q % piece) * 8 : (q % piece) * 8 + 8] = jnp.zeros((8, 128), jnp.float32)

    def exchange(group, order, source, slots, send, recv):
        for r in order:
            m, t = peer(group, r)
            remote(source(r), slots.at[r - 1], send.at[0], recv.at[0], m, t).start()
        m, t = peer(group, 1)
        whole = remote(slots, slots, send.at[0], recv.at[0], m, t)
        whole.wait_recv()
        return whole

    def tree(values):
        while len(values) > 1:
            values = [values[n] + values[n + 1] for n in range(0, len(values), 2)]
        return values[0]

    sent = [exchange(plane, plane_order, lambda r: part.at[a ^ r], got, rs_send, rs_recv)]
    mine[...] = tree([part[a]] + [got[r] for r in range(len(plane_order))])
    sent.append(exchange(depth, depth_order, lambda r: mine, more, ex_send, ex_recv))
    red[...] = tree([mine[...]] + [more[r] for r in range(len(depth_order))])
    sent.append(exchange(plane, plane_order, lambda r: red, last, ag_send, ag_recv))
    sums_ref[a] = red[...]
    for r in plane_order:
        sums_ref[a ^ r] = last[r - 1]

    for copy in halos + obs_copies + pick_copies + sent:
        copy.wait_send()
    for copy in outs:
        copy.wait()


def dot(left, right):
    return jnp.dot(left, right, precision=HIGHEST, preferred_element_type=jnp.float32)


def solve(piece, sums_ref, waves_ref, field_ref, rows_ref, part_ref, advanced_ref, stack, system, lines, rows, wave_at, power_at, sem):
    me = lax.axis_index("member")
    keep = pltpu.make_async_copy(field_ref, advanced_ref, sem.at[0])
    keep.start()
    load = pltpu.make_async_copy(rows_ref, rows, sem.at[1])
    load.start()

    def iota(shape, axis):
        return lax.broadcasted_iota(jnp.int32, shape, axis)

    waves = [waves_ref[j] for j in range(MODES)]
    for j in range(MODES):
        wave_at[j] = 0
        power_at[j] = 0.0
    count = jnp.int32(0)
    for j in range(MODES):
        power = jnp.float32(0.0)
        fresh = jnp.bool_(True)
        for i in range(MODES):
            same = waves[i] == waves[j]
            power = power + jnp.where(same, 1.0 / (1.0 + i), 0.0)
            if i < j:
                fresh = jnp.logical_and(fresh, jnp.logical_not(same))

        @pl.when(fresh)
        def _(count=count, j=j, power=power):
            wave_at[count] = waves[j]
            power_at[count] = power

        count = count + fresh.astype(jnp.int32)

    def cosines(wave, level):
        turn = (wave * (2 * level + 1)) & 63
        turn = jnp.where(turn > 32, 64 - turn, turn)
        back = turn > 16
        turn = jnp.where(back, 32 - turn, turn)
        angle = turn.astype(jnp.float32) * (math.pi / 32.0)
        square = angle * angle
        value = jnp.full(square.shape, 1.0 / math.factorial(14), jnp.float32)
        for n in (12, 10, 8, 6, 4, 2, 0):
            value = 1.0 / math.factorial(n) - value * square
        return jnp.where(back, -value, value)

    level = iota((LEV, 128), 0)
    lane = iota((LEV, 128), 1)
    columns = []
    for i in range(MODES):
        wave = jnp.full((LEV, 128), wave_at[i], jnp.int32)
        columns.append(jnp.sqrt(jnp.full((LEV, 128), power_at[i], jnp.float32)) * cosines(wave, level))
    across = []
    for c in range(4):
        value = jnp.where(lane < 40, columns[3 * c], jnp.where(lane < 80, columns[3 * c + 1], columns[3 * c + 2]))
        across.append(jnp.where(lane < BLOCK, value, 1.0 if c == 3 else 0.0))

    segment = iota((MEMBERS, 128), 1)
    seg0 = segment < 40
    seg1 = segment < 80
    seg2 = segment < BLOCK
    for t in range(6):
        tile = jnp.concatenate(
            [
                sums_ref[(s * 6 + t) // piece, ((s * 6 + t) % piece) * 8 : ((s * 6 + t) % piece) * 8 + 8]
                for s in range(5)
            ],
            axis=0,
        )
        shifts = {0: tile}
        for d in (1, 2, -1, -2) if t < 5 else (1, 2):
            shifts[d] = pltpu.roll(tile, (40 * d) % 128, 1)
        for u in range(3 if t < 5 else 1):
            last = tile if u == 0 else pltpu.roll(tile, 128 - u, 1)
            stack[3 * t + u] = jnp.where(
                seg0, shifts[-u], jnp.where(seg1, shifts[1 - u], jnp.where(seg2, shifts[2 - u], last))
            )

    row = iota((MEMBERS, 128), 0)
    for i in range(MODES):

        @pl.when(i < count)
        def _(i=i):
            totals = [jnp.zeros((MEMBERS, 128), jnp.float32) for _ in range(4)]
            for c in range(4):
                if c == i // 3:
                    totals[c] = jnp.where(segment == row + 40 * (i % 3), 1.0, 0.0)
            factors = [columns[i] * across[c] for c in range(4)]
            for l in range(LEV):
                gram = stack[l]
                for c in range(4):
                    totals[c] = totals[c] + gram * factors[c][l : l + 1]
            for c in range(4):
                system[i * MEMBERS : (i + 1) * MEMBERS, c * 128 : (c + 1) * 128] = totals[c]

    lines[...] = jnp.zeros(lines.shape, jnp.float32)
    wide = (8, 128)
    sub = iota(wide, 0)

    def spread(x):
        return jnp.broadcast_to(x, wide)

    def clear(s, rows_at, first):
        if rows_at.stop <= rows_at.start:
            return
        c0 = s // 3
        cols = slice(first * 128, 512)
        system[rows_at, cols] = system[rows_at, cols] - dot(
            system[rows_at, c0 * 128 : (c0 + 1) * 128], lines[s % 2, :, cols]
        )

    def deferred(s, first):
        clear(s, slice(0, s * MEMBERS), first)
        clear(s, slice((s + 2) * MEMBERS, MODES * MEMBERS), first)

    def eliminate(s):
        c0, offset = s // 3, (s % 3) * MEMBERS
        tiles = list(range(c0, 4))
        base = s * MEMBERS
        vals = {
            (t, c): system[base + 8 * t : base + 8 * t + 8, c * 128 : (c + 1) * 128] for t in range(5) for c in tiles
        }
        if s > 0:
            deferred(s - 1, c0)
        for p in range(5):
            at = [offset + 8 * p + j for j in range(8)]
            cols = [spread(vals[p, c0][:, a : a + 1]) for a in at]
            others = {
                t: [spread(vals[t, c0][:, a : a + 1]) for a in at] for t in [(p + d) % 5 for d in range(1, 5)]
            }
            pivot = [vals[p, c] for c in tiles]
            for j in range(0, 8, 2):
                c1, c2 = cols[j], cols[j + 1]
                a, b = spread(c1[j : j + 1]), spread(c2[j : j + 1])
                b2, d = spread(c1[j + 1 : j + 2]), spread(c2[j + 1 : j + 2])
                inv = 1.0 / (a * d - b * b2)
                a, b, b2, d = a * inv, b * inv, b2 * inv, d * inv
                s1, s2 = sub == j, sub == j + 1
                m1, m2 = jnp.where(s1 | s2, 0.0, c1), jnp.where(s1 | s2, 0.0, c2)

                def step(v):
                    r1, r2 = spread(v[j : j + 1]), spread(v[j + 1 : j + 2])
                    l1, l2 = d * r1 - b * r2, a * r2 - b2 * r1
                    return jnp.where(s1, l1, jnp.where(s2, l2, v - (m1 * l1 + m2 * l2)))

                cols[j + 2 :] = [step(v) for v in cols[j + 2 :]]
                pivot = [step(v) for v in pivot]
            for n, c in enumerate(tiles):
                vals[p, c] = pivot[n]
                line = [spread(pivot[n][j : j + 1]) for j in range(8)]
                for t, multipliers in others.items():
                    prods = [multipliers[j] * line[j] for j in range(8)]
                    while len(prods) > 1:
                        prods = [prods[k] + prods[k + 1] for k in range(0, len(prods), 2)]
                    vals[t, c] = vals[t, c] - prods[0]
        if s >= 2:
            before = ((s - 2) % 3) * MEMBERS
            lines[s % 2, before : before + MEMBERS] = jnp.zeros((MEMBERS, 512), jnp.float32)
        for (t, c), v in vals.items():
            system[base + 8 * t : base + 8 * t + 8, c * 128 : (c + 1) * 128] = v
            lines[s % 2, offset + 8 * t : offset + 8 * t + 8, c * 128 : (c + 1) * 128] = v
        if s + 1 < MODES:
            clear(s, slice((s + 1) * MEMBERS, (s + 2) * MEMBERS), c0)

    for s in range(MODES):

        @pl.when(s < count)
        def _(s=s):
            eliminate(s)

    for s in range(1, MODES):

        @pl.when(s + 1 == count)
        def _(s=s):
            clear(s, slice(0, s * MEMBERS), 3)

    total = jnp.zeros((LOCAL, LEV, 128), jnp.float32)
    load.wait()
    for i in range(MODES):
        weight = jnp.broadcast_to(
            system[i * MEMBERS : (i + 1) * MEMBERS, 384:512][:, BLOCK : BLOCK + 1], (MEMBERS, 128)
        )
        weight = (weight - jnp.sum(weight, axis=0, keepdims=True) * (1.0 / MEMBERS)) * (
            1.0 / math.sqrt(MEMBERS - 1.0)
        )
        stack[i, :MEMBERS] = weight
    for i in range(MODES):

        @pl.when(i >= count)
        def _(i=i):
            stack[i, :MEMBERS] = jnp.zeros((MEMBERS, 128), jnp.float32)

    parts = []
    for k in range(LOCAL):
        total = jnp.zeros((LEV, 128), jnp.float32)
        for i in range(MODES):
            total = total + columns[i] * stack[i, pl.ds(me * LOCAL + k, 1)]
        parts.append(total)

    def add_up(x, _):
        total = jnp.zeros((LEV, CY), jnp.float32)
        for k in range(LOCAL):
            total = total + rows[x, k * LEV : (k + 1) * LEV] * parts[k]
        part_ref[x] = total
        return 0

    lax.fori_loop(0, X, add_up, 0)
    keep.wait()


def finish(share_ref, out_ref, got, send_sem, recv_sem):
    me = lax.axis_index("member")
    tile = lax.axis_index("tile")
    barrier = pltpu.get_barrier_semaphore()
    for r in (2, 1, 3):
        pl.semaphore_signal(barrier, 1, device_id={"member": me ^ r, "tile": tile}, device_id_type=MESH)
    pl.semaphore_wait(barrier, GROUP - 1)
    copies = []
    for r in (2, 1, 3):
        to = me ^ r
        copy = remote(
            share_ref.at[pl.ds(to * RUN, RUN)], got.at[r - 1], send_sem.at[r - 1], recv_sem.at[r - 1], to, tile
        )
        copy.start()
        copies.append(copy)
    for copy in copies:
        copy.wait_recv()
    for x in range(RUN):
        out_ref[:, x * CY : (x + 1) * CY] = (share_ref[me * RUN + x] + got[0, x]) + (got[1, x] + got[2, x])
    for copy in copies:
        copy.wait_send()


def on_device(member_state, courant, obs_col, obs_lev, innovation, obs_var, mode_waves):
    tiles = lax.axis_size("tile")
    n_z = tiles // (N_Y * N_CORE)
    plane = ((2, None), (N_Y.bit_length() - 1, 1))
    depth = ((n_z.bit_length() - 1, N_Y.bit_length()), (1, 0))
    g1 = GROUP * N_Y
    g2 = n_z * N_CORE
    piece = -(-TILES // g1)
    f32 = jnp.float32
    dma = pltpu.SemaphoreType.DMA
    shape = member_state.shape
    field, rows, sums = pl.pallas_call(
        functools.partial(front, plane, depth, piece),
        out_shape=[
            jax.ShapeDtypeStruct((ROWS * X, CY), f32),
            jax.ShapeDtypeStruct((X, ROWS, CY), f32),
            jax.ShapeDtypeStruct((g1, piece * 8, 128), f32),
        ],
        in_specs=[ANY] * 6,
        out_specs=[ANY, ANY, VMEM],
        scratch_shapes=[
            pltpu.VMEM((ROWS * X, CY), f32),
            pltpu.VMEM((2 * LEV * X, CY), f32),
            pltpu.VMEM((X + 4, ROWS, CY), f32),
            pltpu.VMEM((X + 2, ROWS, CY), f32),
            pltpu.VMEM((X, ROWS, CY), f32),
            pltpu.VMEM((X + 2, 2 * LEV, CY), f32),
            pltpu.VMEM((ROWS * X, CY), f32),
            pltpu.VMEM((1, NOBS), jnp.int32),
            pltpu.VMEM((1, NOBS), jnp.int32),
            pltpu.VMEM((1, NOBS), f32),
            pltpu.VMEM((1, NOBS), f32),
            pltpu.VMEM((GROUP, 8, NOBS), jnp.int32),
            pltpu.VMEM((GROUP - 1, 16, NOBS), f32),
            pltpu.VMEM((GROUP, 16, NOBS), f32),
            pltpu.VMEM((WIDE, NOBS), f32),
            pltpu.VMEM((g1, piece * 8, 128), f32),
            pltpu.VMEM((g1 - 1, piece * 8, 128), f32),
            pltpu.VMEM((piece * 8, 128), f32),
            pltpu.VMEM((piece * 8, 128), f32),
            pltpu.VMEM((g2 - 1, piece * 8, 128), f32),
            pltpu.VMEM((g1 - 1, piece * 8, 128), f32),
            dma((6,)),
            dma((4,)),
            dma((4,)),
            dma((GROUP - 1,)),
            dma((GROUP - 1,)),
            dma((GROUP - 1,)),
            dma((GROUP - 1,)),
            dma((1,)),
            dma((1,)),
            dma((1,)),
            dma((1,)),
            dma((1,)),
            dma((1,)),
            dma((2,)),
        ],
        compiler_params=pltpu.CompilerParams(
            collective_id=0, has_side_effects=True, vmem_limit_bytes=VMEM_LIMIT
        ),
        name="front",
    )(
        member_state.reshape(ROWS * X, CY),
        courant.reshape(2 * LEV * X, CY),
        obs_col.reshape(1, NOBS),
        obs_lev.reshape(1, NOBS),
        innovation.reshape(1, NOBS),
        obs_var.reshape(1, NOBS),
    )
    shares, advanced = pl.pallas_call(
        functools.partial(solve, piece),
        out_shape=[
            jax.ShapeDtypeStruct((X, LEV, CY), f32),
            jax.ShapeDtypeStruct((ROWS * X, CY), f32),
        ],
        in_specs=[VMEM, SMEM, ANY, ANY],
        out_specs=[VMEM, ANY],
        scratch_shapes=[
            pltpu.VMEM((LEV, MEMBERS, 128), f32),
            pltpu.VMEM((MODES * MEMBERS, 512), f32),
            pltpu.VMEM((2, 128, 512), f32),
            pltpu.VMEM((X, ROWS, CY), f32),
            pltpu.SMEM((MODES,), jnp.int32),
            pltpu.SMEM((MODES,), f32),
            dma((2,)),
        ],
        compiler_params=pltpu.CompilerParams(vmem_limit_bytes=VMEM_LIMIT),
        name="solve",
    )(sums, mode_waves, field, rows)
    increment = pl.pallas_call(
        finish,
        out_shape=jax.ShapeDtypeStruct((LEV, RUN * CY), f32),
        in_specs=[VMEM],
        out_specs=VMEM,
        scratch_shapes=[
            pltpu.VMEM((GROUP - 1, RUN, LEV, CY), f32),
            dma((GROUP - 1,)),
            dma((GROUP - 1,)),
        ],
        compiler_params=pltpu.CompilerParams(
            collective_id=1, has_side_effects=True, vmem_limit_bytes=VMEM_LIMIT
        ),
        name="finish",
    )(shares)
    return advanced.reshape(shape), increment


def solution(mesh):
    in_specs = (
        P("member", None, "tile", None),
        P(None, None, "tile", None),
        P(("member", "tile")),
        P(("member", "tile")),
        P(("member", "tile")),
        P(("member", "tile")),
        P(),
    )
    out_specs = (P("member", None, "tile", None), P(None, ("member", "tile")))
    return jax.shard_map(
        on_device, mesh=mesh, in_specs=in_specs, out_specs=out_specs, check_vma=False
    )
```

time: 127 us -> 111 us (0.87)
  Pallas kernels: 121 us -> 109 us
  local copies, waits for them, and re-layouts: 4.35 us -> 1.42 us
    pallas_call x1, Pallas kernels: 72.4 us -> 62.3 us  [on_device(): pl.pallas_call(functools.partial(solve, piece), out_shape=[jax.ShapeDtype...]
    pallas_call x1, Pallas kernels: 43.6 us -> 39.9 us  [on_device(): pl.pallas_call(functools.partial(front, plane, depth, piece), out_shape=[...]
    unnamed x13 -> x1, local copies, waits for them, and re-layouts: 4.35 us -> 1.42 us
where the time goes in v2:
time: 111 us
  Pallas kernels  109 us (98%)
  local copies, waits for them, and re-layouts  1.42 us (1%)
    pallas_call x1, Pallas kernels, on_device(): pl.pallas_call(functools.partial(solve, piece), out_shape=[jax.ShapeDtype...  62.3 us
    pallas_call x1, Pallas kernels, on_device(): pl.pallas_call(functools.partial(front, plane, depth, piece), out_shape=[...  39.9 us
    pallas_call x1, Pallas kernels, on_device(): pl.pallas_call(finish, out_shape=jax.ShapeDtypeStruct((LEV, RUN * CY), f3...  6.42 us

profile of v2, /device:TPU:1, one launch (start us, length us, event | category | flops | bytes accessed | tf_op | source)
XLA Modules:
  0.0 110.7 jit_solution(994159202916390968)
XLA Ops:
  0.6 39.9 %front.1 = (f32[3840,128]{1,0:T(8,128)}, f32[24,160,128]{2,1,0:T(8,128)}, f32[16,16,128]{2,1,0:T(8,128)}) custom-call(f32[3840,128]{1,0:T(8,128)} %bitcast.7, f32[768,128]{1,0:T(8,128)} %bitcast.8, s32[1,512]{1,0:T(1,128)} %bitcast.9, s32[1,512]{1,0:T(1,128)} %bitcast.10, f32[1,512]{1,0:T(1,128)} %bitcast.11, f32[1,512]{1,0:T(1,128)} %bitcast.12), custom_call_target="tpu_custom_call" | custom-call | tf_op jit(solution)/shard_map/front/pallas_call | solution.py:565
  40.5 62.3 %solve.1 = (f32[24,16,128]{2,1,0:T(8,128)}, f32[3840,128]{1,0:T(8,128)}) custom-call(f32[16,16,128]{2,1,0:T(8,128)} %get-tuple-element.7.sums_ref, s32[12]{0:T(128)} %waves_ref.1, f32[3840,128]{1,0:T(8,128)} %get-tuple-element.8.field_ref, f32[24,160,128]{2,1,0:T(8,128)} %get-tuple-element.9.rows_ref), custom_call_target="tpu_custom_call" | custom-call | tf_op jit(solution)/shard_map/solve/pallas_call | solution.py:623
  102.8 6.4 %finish.1 = f32[16,768]{1,0:T(8,128)} custom-call(f32[24,16,128]{2,1,0:T(8,128)} %get-tuple-element.11.share_ref), custom_call_target="tpu_custom_call" | custom-call | tf_op jit(solution)/shard_map/finish/pallas_call | solution.py:643
  109.2 1.4 %copy.10 = f32[16,768]{1,0:T(8,128)} copy(f32[16,768]{1,0:T(8,128)} %finish.1) | data formatting | bytes 98304

commit v3 on v2

--- a/solution.py
+++ b/solution.py
@@ -28,7 +28,8 @@
 TILES = 30
 BLOCK = 120
 WIDE = 768
-VMEM_LIMIT = 56 * 1024 * 1024
+PANELS = ((0, 1), (2, 3), (4,))
+VMEM_LIMIT = 48 * 1024 * 1024
 
 
 def remote(src, dst, send, recv, member, tile):
@@ -321,12 +322,10 @@
     return jnp.dot(left, right, precision=HIGHEST, preferred_element_type=jnp.float32)
 
 
-def solve(piece, sums_ref, waves_ref, field_ref, rows_ref, part_ref, advanced_ref, stack, system, lines, rows, wave_at, power_at, sem):
+def solve(piece, sums_ref, waves_ref, field_ref, coeff_ref, advanced_ref, stack, system, lines, field, wave_at, power_at, sem):
     me = lax.axis_index("member")
-    keep = pltpu.make_async_copy(field_ref, advanced_ref, sem.at[0])
-    keep.start()
-    load = pltpu.make_async_copy(rows_ref, rows, sem.at[1])
-    load.start()
+    fetch = pltpu.make_async_copy(field_ref, field, sem.at[0])
+    fetch.start()
 
     def iota(shape, axis):
         return lax.broadcasted_iota(jnp.int32, shape, axis)
@@ -413,6 +412,9 @@
             for c in range(4):
                 system[i * MEMBERS : (i + 1) * MEMBERS, c * 128 : (c + 1) * 128] = totals[c]
 
+    fetch.wait()
+    keep = pltpu.make_async_copy(field, advanced_ref, sem.at[1])
+    keep.start()
     lines[...] = jnp.zeros(lines.shape, jnp.float32)
     wide = (8, 128)
     sub = iota(wide, 0)
@@ -442,34 +444,36 @@
         }
         if s > 0:
             deferred(s - 1, c0)
-        for p in range(5):
-            at = [offset + 8 * p + j for j in range(8)]
-            cols = [spread(vals[p, c0][:, a : a + 1]) for a in at]
-            others = {
-                t: [spread(vals[t, c0][:, a : a + 1]) for a in at] for t in [(p + d) % 5 for d in range(1, 5)]
-            }
-            pivot = [vals[p, c] for c in tiles]
-            for j in range(0, 8, 2):
-                c1, c2 = cols[j], cols[j + 1]
-                a, b = spread(c1[j : j + 1]), spread(c2[j : j + 1])
-                b2, d = spread(c1[j + 1 : j + 2]), spread(c2[j + 1 : j + 2])
+        for panel in PANELS:
+            at = [offset + 8 * panel[0] + j for j in range(8 * len(panel))]
+            cols = [{t: spread(vals[t, c0][:, n : n + 1]) for t in panel} for n in at]
+            after = [(panel[-1] + d) % 5 for d in range(1, 6 - len(panel))]
+            others = {t: [spread(vals[t, c0][:, n : n + 1]) for n in at] for t in after}
+            pivot = [{t: vals[t, c] for t in panel} for c in tiles]
+            for n in range(0, len(at), 2):
+                home, j = panel[n // 8], n % 8
+                c1, c2 = cols[n], cols[n + 1]
+                a, b = spread(c1[home][j : j + 1]), spread(c2[home][j : j + 1])
+                b2, d = spread(c1[home][j + 1 : j + 2]), spread(c2[home][j + 1 : j + 2])
                 inv = 1.0 / (a * d - b * b2)
                 a, b, b2, d = a * inv, b * inv, b2 * inv, d * inv
                 s1, s2 = sub == j, sub == j + 1
-                m1, m2 = jnp.where(s1 | s2, 0.0, c1), jnp.where(s1 | s2, 0.0, c2)
 
                 def step(v):
-                    r1, r2 = spread(v[j : j + 1]), spread(v[j + 1 : j + 2])
+                    r1, r2 = spread(v[home][j : j + 1]), spread(v[home][j + 1 : j + 2])
                     l1, l2 = d * r1 - b * r2, a * r2 - b2 * r1
-                    return jnp.where(s1, l1, jnp.where(s2, l2, v - (m1 * l1 + m2 * l2)))
-
-                cols[j + 2 :] = [step(v) for v in cols[j + 2 :]]
+                    new = {t: v[t] - (c1[t] * l1 + c2[t] * l2) for t in panel}
+                    new[home] = jnp.where(s1, l1, jnp.where(s2, l2, new[home]))
+                    return new
+
+                cols[n + 2 :] = [step(v) for v in cols[n + 2 :]]
                 pivot = [step(v) for v in pivot]
             for n, c in enumerate(tiles):
-                vals[p, c] = pivot[n]
-                line = [spread(pivot[n][j : j + 1]) for j in range(8)]
+                line = [spread(pivot[n][panel[j // 8]][j % 8 : j % 8 + 1]) for j in range(len(at))]
+                for t in panel:
+                    vals[t, c] = pivot[n][t]
                 for t, multipliers in others.items():
-                    prods = [multipliers[j] * line[j] for j in range(8)]
+                    prods = [multipliers[j] * line[j] for j in range(len(at))]
                     while len(prods) > 1:
                         prods = [prods[k] + prods[k + 1] for k in range(0, len(prods), 2)]
                     vals[t, c] = vals[t, c] - prods[0]
@@ -494,8 +498,6 @@
         def _(s=s):
             clear(s, slice(0, s * MEMBERS), 3)
 
-    total = jnp.zeros((LOCAL, LEV, 128), jnp.float32)
-    load.wait()
     for i in range(MODES):
         weight = jnp.broadcast_to(
             system[i * MEMBERS : (i + 1) * MEMBERS, 384:512][:, BLOCK : BLOCK + 1], (MEMBERS, 128)
@@ -510,43 +512,45 @@
         def _(i=i):
             stack[i, :MEMBERS] = jnp.zeros((MEMBERS, 128), jnp.float32)
 
-    parts = []
     for k in range(LOCAL):
         total = jnp.zeros((LEV, 128), jnp.float32)
         for i in range(MODES):
             total = total + columns[i] * stack[i, pl.ds(me * LOCAL + k, 1)]
-        parts.append(total)
-
-    def add_up(x, _):
-        total = jnp.zeros((LEV, CY), jnp.float32)
-        for k in range(LOCAL):
-            total = total + rows[x, k * LEV : (k + 1) * LEV] * parts[k]
-        part_ref[x] = total
-        return 0
-
-    lax.fori_loop(0, X, add_up, 0)
+        coeff_ref[k] = total
     keep.wait()
 
 
-def finish(share_ref, out_ref, got, send_sem, recv_sem):
+def finish(coeff_ref, rows_ref, out_ref, rows, part, got, load_sem, send_sem, recv_sem):
     me = lax.axis_index("member")
     tile = lax.axis_index("tile")
     barrier = pltpu.get_barrier_semaphore()
     for r in (2, 1, 3):
         pl.semaphore_signal(barrier, 1, device_id={"member": me ^ r, "tile": tile}, device_id_type=MESH)
-    pl.semaphore_wait(barrier, GROUP - 1)
+    load = pltpu.make_async_copy(rows_ref, rows, load_sem)
+    load.start()
+
+    def run_for(owner, slot):
+        for x in range(RUN):
+            total = jnp.zeros((LEV, CY), jnp.float32)
+            for k in range(LOCAL):
+                total = total + rows[owner * RUN + x, k * LEV : (k + 1) * LEV] * coeff_ref[k]
+            part[slot, x] = total
+
+    load.wait()
     copies = []
     for r in (2, 1, 3):
         to = me ^ r
-        copy = remote(
-            share_ref.at[pl.ds(to * RUN, RUN)], got.at[r - 1], send_sem.at[r - 1], recv_sem.at[r - 1], to, tile
-        )
+        run_for(to, r)
+        if not copies:
+            pl.semaphore_wait(barrier, GROUP - 1)
+        copy = remote(part.at[r], got.at[r - 1], send_sem.at[r - 1], recv_sem.at[r - 1], to, tile)
         copy.start()
         copies.append(copy)
+    run_for(me, 0)
     for copy in copies:
         copy.wait_recv()
     for x in range(RUN):
-        out_ref[:, x * CY : (x + 1) * CY] = (share_ref[me * RUN + x] + got[0, x]) + (got[1, x] + got[2, x])
+        out_ref[:, x * CY : (x + 1) * CY] = (part[0, x] + got[0, x]) + (got[1, x] + got[2, x])
     for copy in copies:
         copy.wait_send()
 
@@ -620,33 +624,36 @@
         innovation.reshape(1, NOBS),
         obs_var.reshape(1, NOBS),
     )
-    shares, advanced = pl.pallas_call(
+    coeffs, advanced = pl.pallas_call(
         functools.partial(solve, piece),
         out_shape=[
-            jax.ShapeDtypeStruct((X, LEV, CY), f32),
+            jax.ShapeDtypeStruct((LOCAL, LEV, CY), f32),
             jax.ShapeDtypeStruct((ROWS * X, CY), f32),
         ],
-        in_specs=[VMEM, SMEM, ANY, ANY],
+        in_specs=[VMEM, SMEM, ANY],
         out_specs=[VMEM, ANY],
         scratch_shapes=[
             pltpu.VMEM((LEV, MEMBERS, 128), f32),
             pltpu.VMEM((MODES * MEMBERS, 512), f32),
             pltpu.VMEM((2, 128, 512), f32),
-            pltpu.VMEM((X, ROWS, CY), f32),
+            pltpu.VMEM((ROWS * X, CY), f32),
             pltpu.SMEM((MODES,), jnp.int32),
             pltpu.SMEM((MODES,), f32),
             dma((2,)),
         ],
         compiler_params=pltpu.CompilerParams(vmem_limit_bytes=VMEM_LIMIT),
         name="solve",
-    )(sums, mode_waves, field, rows)
+    )(sums, mode_waves, field)
     increment = pl.pallas_call(
         finish,
         out_shape=jax.ShapeDtypeStruct((LEV, RUN * CY), f32),
-        in_specs=[VMEM],
+        in_specs=[VMEM, ANY],
         out_specs=VMEM,
         scratch_shapes=[
+            pltpu.VMEM((X, ROWS, CY), f32),
+            pltpu.VMEM((GROUP, RUN, LEV, CY), f32),
             pltpu.VMEM((GROUP - 1, RUN, LEV, CY), f32),
+            dma,
             dma((GROUP - 1,)),
             dma((GROUP - 1,)),
         ],
@@ -654,7 +661,7 @@
             collective_id=1, has_side_effects=True, vmem_limit_bytes=VMEM_LIMIT
         ),
         name="finish",
-    )(shares)
+    )(coeffs, rows)
     return advanced.reshape(shape), increment
 
 

time: 111 us -> 64.3 us (0.58)
  Pallas kernels: 109 us -> 59.1 us
  local copies, waits for them, and re-layouts: 1.42 us -> 4.35 us
    pallas_call x1, Pallas kernels: 62.3 us -> 14.5 us  [on_device(): pl.pallas_call(functools.partial(solve, piece), out_shape=[jax.ShapeDtype...]
    unnamed x1 -> x13, local copies, waits for them, and re-layouts: 1.42 us -> 4.35 us
    pallas_call x1, Pallas kernels: 6.42 us -> 5.01 us  [on_device(): pl.pallas_call(finish, out_shape=jax.ShapeDtypeStruct((LEV, RUN * CY), f3...]
where the time goes in v3:
time: 64.3 us; the launch traced here: 64.1 us
  Pallas kernels  59.1 us (92%)
  local copies, waits for them, and re-layouts  4.35 us (7%)
  between operations  0.68 us (1%)
    pallas_call x1, Pallas kernels, on_device(): pl.pallas_call(functools.partial(front, plane, depth, piece), out_shape=[...  39.6 us
    pallas_call x1, Pallas kernels, on_device(): pl.pallas_call(functools.partial(solve, piece), out_shape=[jax.ShapeDtype...  14.5 us
    pallas_call x1, Pallas kernels, on_device(): pl.pallas_call(finish, out_shape=jax.ShapeDtypeStruct((LEV, RUN * CY), f3...  5.01 us
    unnamed x13, local copies, waits for them, and re-layouts  4.35 us

profile of v3, /device:TPU:1, one launch (start us, length us, event | category | flops | bytes accessed | tf_op | source)
XLA Modules:
  0.0 64.1 jit_solution(16925774815020770505)
XLA Ops:
  0.6 0.0 copy-start.5
  0.6 0.0 copy-start
  0.7 1.0 %copy-done = f32[2,16,24,128]{3,2,1,0:T(8,128)S(1)} copy-done((f32[2,16,24,128]{3,2,1,0:T(8,128)S(1)}, f32[2,16,24,128]{3,2,1,0:T(8,128)}, u32[]{:S(2)}) %copy-start) | copy-done | bytes 393240
  1.6 0.0 copy-start.1
  1.6 0.7 %copy-done.1 = s32[512]{0:T(512)S(1)} copy-done((s32[512]{0:T(512)S(1)}, s32[512]{0:T(512)}, u32[]{:S(2)}) %copy-start.1) | copy-done | bytes 2072
  2.3 0.0 copy-start.2
  2.3 0.7 %copy-done.2 = s32[512]{0:T(512)S(1)} copy-done((s32[512]{0:T(512)S(1)}, s32[512]{0:T(512)}, u32[]{:S(2)}) %copy-start.2) | copy-done | bytes 2072
  3.0 0.0 copy-start.3
  3.0 0.7 %copy-done.3 = f32[512]{0:T(512)S(1)} copy-done((f32[512]{0:T(512)S(1)}, f32[512]{0:T(512)}, u32[]{:S(2)}) %copy-start.3) | copy-done | bytes 2072
  3.7 0.0 copy-start.4
  3.7 0.7 %copy-done.4 = f32[512]{0:T(512)S(1)} copy-done((f32[512]{0:T(512)S(1)}, f32[512]{0:T(512)}, u32[]{:S(2)}) %copy-start.4) | copy-done | bytes 2072
  4.4 39.6 %front.1 = (f32[3840,128]{1,0:T(8,128)S(1)}, f32[24,160,128]{2,1,0:T(8,128)S(1)}, f32[16,16,128]{2,1,0:T(8,128)S(1)}) custom-call(f32[3840,128]{1,0:T(8,128)} %bitcast.12, f32[768,128]{1,0:T(8,128)S(1)} %bitcast.7, s32[1,512]{1,0:T(1,128)S(1)} %bitcast.8, s32[1,512]{1,0:T(1,128)S(1)} %bitcast.9, f32[1,512]{1,0:T(1,128)S(1)} %bitcast.10, f32[1,512]{1,0:T(1,128)S(1)} %bitcast.11), custom_call_target="tpu_custom_call" | custom-call | tf_op jit(solution)/shard_map/front/pallas_call | solution.py:569
  44.0 0.0 copy-done.5
  44.0 14.5 %solve.1 = (f32[10,16,128]{2,1,0:T(8,128)S(1)}, f32[3840,128]{1,0:T(8,128)}) custom-call(f32[16,16,128]{2,1,0:T(8,128)S(1)} %get-tuple-element.7.sums_ref, s32[12]{0:T(128)S(1)} %copy-done.5, f32[3840,128]{1,0:T(8,128)S(1)} %get-tuple-element.8.field_ref), custom_call_target="tpu_custom_call" | custom-call | tf_op jit(solution)/shard_map/solve/pallas_call | solution.py:627
  58.5 5.0 %finish.1 = f32[16,768]{1,0:T(8,128)S(1)} custom-call(f32[10,16,128]{2,1,0:T(8,128)S(1)} %get-tuple-element.10.coeff_ref, f32[24,160,128]{2,1,0:T(8,128)S(1)} %get-tuple-element.11.rows_ref), custom_call_target="tpu_custom_call" | custom-call | tf_op jit(solution)/shard_map/finish/pallas_call | solution.py:647
  63.5 0.6 copy.10
Async XLA Ops:
  0.6 43.3 %copy-start.5 = (s32[12]{0:T(128)S(1)}, s32[12]{0:T(128)}, u32[]{:S(2)}) copy-start(s32[12]{0:T(128)} %waves_ref.1) | copy-start | bytes 148
  0.6 1.0 %copy-start = (f32[2,16,24,128]{3,2,1,0:T(8,128)S(1)}, f32[2,16,24,128]{3,2,1,0:T(8,128)}, u32[]{:S(2)}) copy-start(f32[2,16,24,128]{3,2,1,0:T(8,128)} %param.8) | copy-start | bytes 1179652
  1.6 0.7 %copy-start.1 = (s32[512]{0:T(512)S(1)}, s32[512]{0:T(512)}, u32[]{:S(2)}) copy-start(s32[512]{0:T(512)} %param.9) | copy-start | bytes 6148
  2.3 0.7 %copy-start.2 = (s32[512]{0:T(512)S(1)}, s32[512]{0:T(512)}, u32[]{:S(2)}) copy-start(s32[512]{0:T(512)} %param.10) | copy-start | bytes 6148
  3.0 0.7 %copy-start.3 = (f32[512]{0:T(512)S(1)}, f32[512]{0:T(512)}, u32[]{:S(2)}) copy-start(f32[512]{0:T(512)} %param.11) | copy-start | bytes 6148
  3.7 0.7 %copy-start.4 = (f32[512]{0:T(512)S(1)}, f32[512]{0:T(512)}, u32[]{:S(2)}) copy-start(f32[512]{0:T(512)} %param.12) | copy-start | bytes 6148

commit v4 on v3

--- a/solution.py
+++ b/solution.py
@@ -28,8 +28,11 @@
 TILES = 30
 BLOCK = 120
 WIDE = 768
-PANELS = ((0, 1), (2, 3), (4,))
-VMEM_LIMIT = 48 * 1024 * 1024
+AHEAD = 8
+PANELS = ((0,), (1,), (2,), (3,), (4,))
+FRONT_VMEM = 56 * 1024 * 1024
+SOLVE_VMEM = 53 * 1024 * 1024
+FINISH_VMEM = 52 * 1024 * 1024
 
 
 def remote(src, dst, send, recv, member, tile):
@@ -210,12 +213,16 @@
         field[pl.ds(i, ROWS, stride=X), :] = q2[i]
         return 0
 
-    lax.fori_loop(2, X, first, 0, unroll=2)
+    for i in (2, X - 1):
+        first(i, 0)
+    lax.fori_loop(3, X - 1, first, 0, unroll=4)
+    lax.fori_loop(2, X - 2, second, 0, unroll=4)
     for copy in halos:
         copy.wait_recv()
     for i in (0, 1, X, X + 1):
         first(i, 0)
-    lax.fori_loop(0, X, second, 0, unroll=4)
+    for i in (0, 1, X - 2, X - 1):
+        second(i, 0)
 
     outs = [pltpu.make_async_copy(q2, rows_out, out_sem.at[1])]
     outs[0].start()
@@ -322,8 +329,10 @@
     return jnp.dot(left, right, precision=HIGHEST, preferred_element_type=jnp.float32)
 
 
-def solve(piece, sums_ref, waves_ref, field_ref, coeff_ref, advanced_ref, stack, system, lines, field, wave_at, power_at, sem):
+def solve(piece, sums_in, waves_ref, field_ref, coeff_ref, advanced_ref, sums_ref, stack, system, lines, field, wave_at, power_at, sem):
     me = lax.axis_index("member")
+    take = pltpu.make_async_copy(sums_in, sums_ref, sem.at[2])
+    take.start()
     fetch = pltpu.make_async_copy(field_ref, field, sem.at[0])
     fetch.start()
 
@@ -378,6 +387,7 @@
     seg0 = segment < 40
     seg1 = segment < 80
     seg2 = segment < BLOCK
+    take.wait()
     for t in range(6):
         tile = jnp.concatenate(
             [
@@ -432,24 +442,30 @@
         )
 
     def deferred(s, first):
+        edges = [(s + 1) * MEMBERS + AHEAD, (s + 2) * MEMBERS, (s + 3) * MEMBERS, MODES * MEMBERS]
+        for start, stop in zip(edges[:-1], edges[1:]):
+            clear(s, slice(start, min(stop, MODES * MEMBERS)), first)
         clear(s, slice(0, s * MEMBERS), first)
-        clear(s, slice((s + 2) * MEMBERS, MODES * MEMBERS), first)
 
     def eliminate(s):
         c0, offset = s // 3, (s % 3) * MEMBERS
         tiles = list(range(c0, 4))
         base = s * MEMBERS
-        vals = {
-            (t, c): system[base + 8 * t : base + 8 * t + 8, c * 128 : (c + 1) * 128] for t in range(5) for c in tiles
-        }
+        extra = list(range(5, 5 + AHEAD // 8)) if s + 1 < MODES else []
+
+        def spot(t, c):
+            return slice(base + 8 * t, base + 8 * t + 8), slice(c * 128, (c + 1) * 128)
+
+        if s >= 2:
+            before = ((s - 2) % 3) * MEMBERS
+            lines[s % 2, before : before + MEMBERS] = jnp.zeros((MEMBERS, 512), jnp.float32)
         if s > 0:
             deferred(s - 1, c0)
         for panel in PANELS:
             at = [offset + 8 * panel[0] + j for j in range(8 * len(panel))]
-            cols = [{t: spread(vals[t, c0][:, n : n + 1]) for t in panel} for n in at]
-            after = [(panel[-1] + d) % 5 for d in range(1, 6 - len(panel))]
-            others = {t: [spread(vals[t, c0][:, n : n + 1]) for n in at] for t in after}
-            pivot = [{t: vals[t, c] for t in panel} for c in tiles]
+            pivot = [{t: system[spot(t, c)] for t in panel} for c in tiles]
+            cols = [{t: spread(pivot[0][t][:, n : n + 1]) for t in panel} for n in at]
+            after = [(panel[-1] + d) % 5 for d in range(1, 6 - len(panel))] + extra
             for n in range(0, len(at), 2):
                 home, j = panel[n // 8], n % 8
                 c1, c2 = cols[n], cols[n + 1]
@@ -468,23 +484,23 @@
 
                 cols[n + 2 :] = [step(v) for v in cols[n + 2 :]]
                 pivot = [step(v) for v in pivot]
+            line = {}
             for n, c in enumerate(tiles):
-                line = [spread(pivot[n][panel[j // 8]][j % 8 : j % 8 + 1]) for j in range(len(at))]
                 for t in panel:
-                    vals[t, c] = pivot[n][t]
-                for t, multipliers in others.items():
-                    prods = [multipliers[j] * line[j] for j in range(len(at))]
+                    system[spot(t, c)] = pivot[n][t]
+                for j in range(len(at)):
+                    line[c, j] = spread(pivot[n][panel[j // 8]][j % 8 : j % 8 + 1])
+            for t in after:
+                head = system[spot(t, c0)]
+                multipliers = [spread(head[:, n : n + 1]) for n in at]
+                for c in tiles:
+                    prods = [multipliers[j] * line[c, j] for j in range(len(at))]
                     while len(prods) > 1:
                         prods = [prods[k] + prods[k + 1] for k in range(0, len(prods), 2)]
-                    vals[t, c] = vals[t, c] - prods[0]
-        if s >= 2:
-            before = ((s - 2) % 3) * MEMBERS
-            lines[s % 2, before : before + MEMBERS] = jnp.zeros((MEMBERS, 512), jnp.float32)
-        for (t, c), v in vals.items():
-            system[base + 8 * t : base + 8 * t + 8, c * 128 : (c + 1) * 128] = v
-            lines[s % 2, offset + 8 * t : offset + 8 * t + 8, c * 128 : (c + 1) * 128] = v
-        if s + 1 < MODES:
-            clear(s, slice((s + 1) * MEMBERS, (s + 2) * MEMBERS), c0)
+                    system[spot(t, c)] = system[spot(t, c)] - prods[0]
+        for t in range(5):
+            for c in tiles:
+                lines[s % 2, offset + 8 * t : offset + 8 * t + 8, c * 128 : (c + 1) * 128] = system[spot(t, c)]
 
     for s in range(MODES):
 
@@ -520,14 +536,18 @@
     keep.wait()
 
 
-def finish(coeff_ref, rows_ref, out_ref, rows, part, got, load_sem, send_sem, recv_sem):
+def finish(coeff_in, rows_ref, out_ref, coeff_ref, rows, part, got, load_sem, send_sem, recv_sem):
     me = lax.axis_index("member")
     tile = lax.axis_index("tile")
     barrier = pltpu.get_barrier_semaphore()
     for r in (2, 1, 3):
         pl.semaphore_signal(barrier, 1, device_id={"member": me ^ r, "tile": tile}, device_id_type=MESH)
-    load = pltpu.make_async_copy(rows_ref, rows, load_sem)
-    load.start()
+    loads = [
+        pltpu.make_async_copy(rows_ref, rows, load_sem.at[0]),
+        pltpu.make_async_copy(coeff_in, coeff_ref, load_sem.at[1]),
+    ]
+    for copy in loads:
+        copy.start()
 
     def run_for(owner, slot):
         for x in range(RUN):
@@ -536,7 +556,8 @@
                 total = total + rows[owner * RUN + x, k * LEV : (k + 1) * LEV] * coeff_ref[k]
             part[slot, x] = total
 
-    load.wait()
+    for copy in loads:
+        copy.wait()
     copies = []
     for r in (2, 1, 3):
         to = me ^ r
@@ -613,7 +634,7 @@
             dma((2,)),
         ],
         compiler_params=pltpu.CompilerParams(
-            collective_id=0, has_side_effects=True, vmem_limit_bytes=VMEM_LIMIT
+            collective_id=0, has_side_effects=True, vmem_limit_bytes=FRONT_VMEM
         ),
         name="front",
     )(
@@ -630,35 +651,37 @@
             jax.ShapeDtypeStruct((LOCAL, LEV, CY), f32),
             jax.ShapeDtypeStruct((ROWS * X, CY), f32),
         ],
-        in_specs=[VMEM, SMEM, ANY],
+        in_specs=[ANY, SMEM, ANY],
         out_specs=[VMEM, ANY],
         scratch_shapes=[
+            pltpu.VMEM(sums.shape, f32),
             pltpu.VMEM((LEV, MEMBERS, 128), f32),
             pltpu.VMEM((MODES * MEMBERS, 512), f32),
             pltpu.VMEM((2, 128, 512), f32),
             pltpu.VMEM((ROWS * X, CY), f32),
             pltpu.SMEM((MODES,), jnp.int32),
             pltpu.SMEM((MODES,), f32),
-            dma((2,)),
+            dma((3,)),
         ],
-        compiler_params=pltpu.CompilerParams(vmem_limit_bytes=VMEM_LIMIT),
+        compiler_params=pltpu.CompilerParams(vmem_limit_bytes=SOLVE_VMEM),
         name="solve",
     )(sums, mode_waves, field)
     increment = pl.pallas_call(
         finish,
         out_shape=jax.ShapeDtypeStruct((LEV, RUN * CY), f32),
-        in_specs=[VMEM, ANY],
+        in_specs=[ANY, ANY],
         out_specs=VMEM,
         scratch_shapes=[
+            pltpu.VMEM((LOCAL, LEV, CY), f32),
             pltpu.VMEM((X, ROWS, CY), f32),
             pltpu.VMEM((GROUP, RUN, LEV, CY), f32),
             pltpu.VMEM((GROUP - 1, RUN, LEV, CY), f32),
-            dma,
+            dma((2,)),
             dma((GROUP - 1,)),
             dma((GROUP - 1,)),
         ],
         compiler_params=pltpu.CompilerParams(
-            collective_id=1, has_side_effects=True, vmem_limit_bytes=VMEM_LIMIT
+            collective_id=1, has_side_effects=True, vmem_limit_bytes=FINISH_VMEM
         ),
         name="finish",
     )(coeffs, rows)

time: 64.3 us -> 61.5 us (0.956)
  local copies, waits for them, and re-layouts: 4.35 us -> 1.52 us
    unnamed x13 -> x5, local copies, waits for them, and re-layouts: 4.35 us -> 1.52 us
    pallas_call x1, Pallas kernels: 14.5 us -> 15.4 us  [on_device(): pl.pallas_call(functools.partial(solve, piece), out_shape=[jax.ShapeDtype...]
    pallas_call x1, Pallas kernels: 39.6 us -> 38.7 us  [on_device(): pl.pallas_call(functools.partial(front, plane, depth, piece), out_shape=[...]
where the time goes in v4:
time: 61.5 us; the launch traced here: 61.3 us
  Pallas kernels  59.1 us (96%)
  local copies, waits for them, and re-layouts  1.52 us (2%)
  between operations  0.68 us (1%)
    pallas_call x1, Pallas kernels, on_device(): pl.pallas_call(functools.partial(front, plane, depth, piece), out_shape=[...  38.7 us
    pallas_call x1, Pallas kernels, on_device(): pl.pallas_call(functools.partial(solve, piece), out_shape=[jax.ShapeDtype...  15.4 us
    pallas_call x1, Pallas kernels, on_device(): pl.pallas_call(finish, out_shape=jax.ShapeDtypeStruct((LEV, RUN * CY), f3...  5.01 us
    unnamed x5, local copies, waits for them, and re-layouts  1.52 us

profile of v4, /device:TPU:1, one launch (start us, length us, event | category | flops | bytes accessed | tf_op | source)
XLA Modules:
  0.0 61.3 jit_solution(12590143441071705524)
XLA Ops:
  0.6 0.0 copy-start.1
  0.6 38.7 %front.1 = (f32[3840,128]{1,0:T(8,128)}, f32[24,160,128]{2,1,0:T(8,128)}, f32[16,16,128]{2,1,0:T(8,128)}) custom-call(f32[3840,128]{1,0:T(8,128)} %bitcast.7, f32[768,128]{1,0:T(8,128)} %bitcast.8, s32[1,512]{1,0:T(1,128)} %bitcast.9, s32[1,512]{1,0:T(1,128)} %bitcast.10, f32[1,512]{1,0:T(1,128)} %bitcast.11, f32[1,512]{1,0:T(1,128)} %bitcast.12), custom_call_target="tpu_custom_call" | custom-call | tf_op jit(solution)/shard_map/front/pallas_call | solution.py:590
  39.3 0.0 copy-done.1
  39.3 0.0 copy-start
  39.3 0.9 %copy-done = f32[16,16,128]{2,1,0:T(8,128)S(1)} copy-done((f32[16,16,128]{2,1,0:T(8,128)S(1)}, f32[16,16,128]{2,1,0:T(8,128)}, u32[]{:S(2)}) %copy-start) | copy-done | bytes 131096
  40.2 15.4 %solve.1 = (f32[10,16,128]{2,1,0:T(8,128)S(1)}, f32[3840,128]{1,0:T(8,128)}) custom-call(f32[16,16,128]{2,1,0:T(8,128)S(1)} %copy-done, s32[12]{0:T(128)S(1)} %copy-done.1, f32[3840,128]{1,0:T(8,128)} %get-tuple-element.8.field_ref), custom_call_target="tpu_custom_call" | custom-call | tf_op jit(solution)/shard_map/solve/pallas_call | solution.py:648
  55.7 5.0 %finish.1 = f32[16,768]{1,0:T(8,128)S(1)} custom-call(f32[10,16,128]{2,1,0:T(8,128)S(1)} %get-tuple-element.10.coeff_in, f32[24,160,128]{2,1,0:T(8,128)} %get-tuple-element.11.rows_ref), custom_call_target="tpu_custom_call" | custom-call | tf_op jit(solution)/shard_map/finish/pallas_call | solution.py:669
  60.7 0.6 %copy.10 = f32[16,768]{1,0:T(8,128)} copy(f32[16,768]{1,0:T(8,128)S(1)} %finish.1) | data formatting | bytes 98304
Async XLA Ops:
  0.6 38.7 %copy-start.1 = (s32[12]{0:T(128)S(1)}, s32[12]{0:T(128)}, u32[]{:S(2)}) copy-start(s32[12]{0:T(128)} %waves_ref.1) | copy-start | bytes 148
  39.3 0.9 %copy-start = (f32[16,16,128]{2,1,0:T(8,128)S(1)}, f32[16,16,128]{2,1,0:T(8,128)}, u32[]{:S(2)}) copy-start(f32[16,16,128]{2,1,0:T(8,128)} %get-tuple-element.7.sums_in) | copy-start | bytes 393220

commit v5 on v4

--- a/solution.py
+++ b/solution.py
@@ -29,7 +29,6 @@
 BLOCK = 120
 WIDE = 768
 AHEAD = 8
-PANELS = ((0,), (1,), (2,), (3,), (4,))
 FRONT_VMEM = 56 * 1024 * 1024
 SOLVE_VMEM = 53 * 1024 * 1024
 FINISH_VMEM = 52 * 1024 * 1024
@@ -96,7 +95,7 @@
     var_in,
     field_out,
     rows_out,
-    sums_ref,
+    sums_out,
     state,
     courant,
     q0,
@@ -118,6 +117,7 @@
     mine,
     more,
     last,
+    sums_ref,
     load_sem,
     halo_send,
     halo_recv,
@@ -199,7 +199,7 @@
         copy.start()
         obs_copies.append(copy)
 
-    lax.fori_loop(2, 22, turn, 0)
+    lax.fori_loop(2, 22, turn, 0, unroll=5)
 
     def first(i, _):
         q1[i] = upwind(q0[i + 1], q0[i], q0[i + 2], wind[i])
@@ -215,8 +215,8 @@
 
     for i in (2, X - 1):
         first(i, 0)
-    lax.fori_loop(3, X - 1, first, 0, unroll=4)
-    lax.fori_loop(2, X - 2, second, 0, unroll=4)
+    lax.fori_loop(3, X - 1, first, 0, unroll=20)
+    lax.fori_loop(2, X - 2, second, 0, unroll=20)
     for copy in halos:
         copy.wait_recv()
     for i in (0, 1, X, X + 1):
@@ -318,6 +318,8 @@
     sums_ref[a] = red[...]
     for r in plane_order:
         sums_ref[a ^ r] = last[r - 1]
+    outs.append(pltpu.make_async_copy(sums_ref, sums_out.at[pl.ds(0, sums_ref.shape[0])], out_sem.at[2]))
+    outs[2].start()
 
     for copy in halos + obs_copies + pick_copies + sent:
         copy.wait_send()
@@ -331,7 +333,7 @@
 
 def solve(piece, sums_in, waves_ref, field_ref, coeff_ref, advanced_ref, sums_ref, stack, system, lines, field, wave_at, power_at, sem):
     me = lax.axis_index("member")
-    take = pltpu.make_async_copy(sums_in, sums_ref, sem.at[2])
+    take = pltpu.make_async_copy(sums_in.at[pl.ds(0, sums_ref.shape[0])], sums_ref, sem.at[2])
     take.start()
     fetch = pltpu.make_async_copy(field_ref, field, sem.at[0])
     fetch.start()
@@ -461,40 +463,40 @@
             lines[s % 2, before : before + MEMBERS] = jnp.zeros((MEMBERS, 512), jnp.float32)
         if s > 0:
             deferred(s - 1, c0)
-        for panel in PANELS:
-            at = [offset + 8 * panel[0] + j for j in range(8 * len(panel))]
-            pivot = [{t: system[spot(t, c)] for t in panel} for c in tiles]
-            cols = [{t: spread(pivot[0][t][:, n : n + 1]) for t in panel} for n in at]
-            after = [(panel[-1] + d) % 5 for d in range(1, 6 - len(panel))] + extra
-            for n in range(0, len(at), 2):
-                home, j = panel[n // 8], n % 8
-                c1, c2 = cols[n], cols[n + 1]
-                a, b = spread(c1[home][j : j + 1]), spread(c2[home][j : j + 1])
-                b2, d = spread(c1[home][j + 1 : j + 2]), spread(c2[home][j + 1 : j + 2])
+        for p in range(5):
+            at = [offset + 8 * p + j for j in range(8)]
+            pivot = [system[spot(p, c)] for c in tiles]
+            cols = [spread(pivot[0][:, n : n + 1]) for n in at]
+            keep_row = swap_row = jnp.zeros(wide, jnp.float32)
+            for j in range(0, 8, 2):
+                c1, c2 = cols[j], cols[j + 1]
+                a, b = spread(c1[j : j + 1]), spread(c2[j : j + 1])
+                b2, d = spread(c1[j + 1 : j + 2]), spread(c2[j + 1 : j + 2])
                 inv = 1.0 / (a * d - b * b2)
-                a, b, b2, d = a * inv, b * inv, b2 * inv, d * inv
                 s1, s2 = sub == j, sub == j + 1
+                m1 = jnp.where(s1 | s2, 0.0, c1 * d - c2 * b2) * inv
+                m2 = jnp.where(s1 | s2, 0.0, c2 * a - c1 * b) * inv
+                keep_row = jnp.where(s1, d * inv, jnp.where(s2, a * inv, keep_row))
+                swap_row = jnp.where(s1, b * inv, jnp.where(s2, b2 * inv, swap_row))
 
                 def step(v):
-                    r1, r2 = spread(v[home][j : j + 1]), spread(v[home][j + 1 : j + 2])
-                    l1, l2 = d * r1 - b * r2, a * r2 - b2 * r1
-                    new = {t: v[t] - (c1[t] * l1 + c2[t] * l2) for t in panel}
-                    new[home] = jnp.where(s1, l1, jnp.where(s2, l2, new[home]))
-                    return new
-
-                cols[n + 2 :] = [step(v) for v in cols[n + 2 :]]
+                    return v - (m1 * spread(v[j : j + 1]) + m2 * spread(v[j + 1 : j + 2]))
+
+                cols[j + 2 :] = [step(v) for v in cols[j + 2 :]]
                 pivot = [step(v) for v in pivot]
             line = {}
             for n, c in enumerate(tiles):
-                for t in panel:
-                    system[spot(t, c)] = pivot[n][t]
-                for j in range(len(at)):
-                    line[c, j] = spread(pivot[n][panel[j // 8]][j % 8 : j % 8 + 1])
-            for t in after:
+                v = pivot[n]
+                swapped = jnp.where(sub % 2 == 0, pltpu.roll(v, 7, 0), pltpu.roll(v, 1, 0))
+                v = keep_row * v - swap_row * swapped
+                system[spot(p, c)] = v
+                for j in range(8):
+                    line[c, j] = spread(v[j : j + 1])
+            for t in [(p + d) % 5 for d in range(1, 5)] + extra:
                 head = system[spot(t, c0)]
                 multipliers = [spread(head[:, n : n + 1]) for n in at]
                 for c in tiles:
-                    prods = [multipliers[j] * line[c, j] for j in range(len(at))]
+                    prods = [multipliers[j] * line[c, j] for j in range(8)]
                     while len(prods) > 1:
                         prods = [prods[k] + prods[k + 1] for k in range(0, len(prods), 2)]
                     system[spot(t, c)] = system[spot(t, c)] - prods[0]
@@ -592,10 +594,10 @@
         out_shape=[
             jax.ShapeDtypeStruct((ROWS * X, CY), f32),
             jax.ShapeDtypeStruct((X, ROWS, CY), f32),
-            jax.ShapeDtypeStruct((g1, piece * 8, 128), f32),
+            jax.ShapeDtypeStruct((16 * g1, piece * 8, 128), f32),
         ],
         in_specs=[ANY] * 6,
-        out_specs=[ANY, ANY, VMEM],
+        out_specs=[ANY, ANY, ANY],
         scratch_shapes=[
             pltpu.VMEM((ROWS * X, CY), f32),
             pltpu.VMEM((2 * LEV * X, CY), f32),
@@ -618,6 +620,7 @@
             pltpu.VMEM((piece * 8, 128), f32),
             pltpu.VMEM((g2 - 1, piece * 8, 128), f32),
             pltpu.VMEM((g1 - 1, piece * 8, 128), f32),
+            pltpu.VMEM((g1, piece * 8, 128), f32),
             dma((6,)),
             dma((4,)),
             dma((4,)),
@@ -631,7 +634,7 @@
             dma((1,)),
             dma((1,)),
             dma((1,)),
-            dma((2,)),
+            dma((3,)),
         ],
         compiler_params=pltpu.CompilerParams(
             collective_id=0, has_side_effects=True, vmem_limit_bytes=FRONT_VMEM
@@ -654,7 +657,7 @@
         in_specs=[ANY, SMEM, ANY],
         out_specs=[VMEM, ANY],
         scratch_shapes=[
-            pltpu.VMEM(sums.shape, f32),
+            pltpu.VMEM((g1, piece * 8, 128), f32),
             pltpu.VMEM((LEV, MEMBERS, 128), f32),
             pltpu.VMEM((MODES * MEMBERS, 512), f32),
             pltpu.VMEM((2, 128, 512), f32),

time: 61.5 us -> 58.8 us (0.956)
  Pallas kernels: 59.1 us -> 57.4 us
  local copies, waits for them, and re-layouts: 1.52 us -> 0.63 us
    pallas_call x1, Pallas kernels: 15.4 us -> 13.7 us  [on_device(): pl.pallas_call(functools.partial(solve, piece), out_shape=[jax.ShapeDtype...]
    unnamed x5 -> x3, local copies, waits for them, and re-layouts: 1.52 us -> 0.63 us
where the time goes in v5:
time: 58.8 us; the launch traced here: 58.7 us
  Pallas kernels  57.4 us (98%)
  between operations  0.67 us (1%)
  local copies, waits for them, and re-layouts  0.63 us (1%)
    pallas_call x1, Pallas kernels, on_device(): pl.pallas_call(functools.partial(front, plane, depth, piece), out_shape=[...  38.6 us
    pallas_call x1, Pallas kernels, on_device(): pl.pallas_call(functools.partial(solve, piece), out_shape=[jax.ShapeDtype...  13.7 us
    pallas_call x1, Pallas kernels, on_device(): pl.pallas_call(finish, out_shape=jax.ShapeDtypeStruct((LEV, RUN * CY), f3...  5.02 us

profile of v5, /device:TPU:1, one launch (start us, length us, event | category | flops | bytes accessed | tf_op | source)
XLA Modules:
  0.0 58.7 jit_solution(14084853980298345984)
XLA Ops:
  0.6 0.0 copy-start
  0.6 38.6 %front.1 = (f32[3840,128]{1,0:T(8,128)}, f32[24,160,128]{2,1,0:T(8,128)}, f32[256,16,128]{2,1,0:T(8,128)}) custom-call(f32[3840,128]{1,0:T(8,128)} %bitcast.7, f32[768,128]{1,0:T(8,128)} %bitcast.8, s32[1,512]{1,0:T(1,128)} %bitcast.9, s32[1,512]{1,0:T(1,128)} %bitcast.10, f32[1,512]{1,0:T(1,128)} %bitcast.11, f32[1,512]{1,0:T(1,128)} %bitcast.12), custom_call_target="tpu_custom_call" | custom-call | tf_op jit(solution)/shard_map/front/pallas_call | solution.py:592
  39.3 0.0 copy-done
  39.3 13.7 %solve.1 = (f32[10,16,128]{2,1,0:T(8,128)S(1)}, f32[3840,128]{1,0:T(8,128)}) custom-call(f32[256,16,128]{2,1,0:T(8,128)} %get-tuple-element.7.sums_in, s32[12]{0:T(128)S(1)} %copy-done, f32[3840,128]{1,0:T(8,128)} %get-tuple-element.8.field_ref), custom_call_target="tpu_custom_call" | custom-call | tf_op jit(solution)/shard_map/solve/pallas_call | solution.py:651
  53.0 5.0 %finish.1 = f32[16,768]{1,0:T(8,128)S(1)} custom-call(f32[10,16,128]{2,1,0:T(8,128)S(1)} %get-tuple-element.10.coeff_in, f32[24,160,128]{2,1,0:T(8,128)} %get-tuple-element.11.rows_ref), custom_call_target="tpu_custom_call" | custom-call | tf_op jit(solution)/shard_map/finish/pallas_call | solution.py:672
  58.0 0.6 %copy.10 = f32[16,768]{1,0:T(8,128)} copy(f32[16,768]{1,0:T(8,128)S(1)} %finish.1) | data formatting | bytes 98304
Async XLA Ops:
  0.6 38.7 %copy-start = (s32[12]{0:T(128)S(1)}, s32[12]{0:T(128)}, u32[]{:S(2)}) copy-start(s32[12]{0:T(128)} %waves_ref.1) | copy-start | bytes 148

commit v6 on v5

--- a/solution.py
+++ b/solution.py
@@ -146,8 +146,8 @@
         return me ^ member, tile ^ shift
 
     loads = [
-        pltpu.make_async_copy(state_ref, state, load_sem.at[0]),
-        pltpu.make_async_copy(courant_ref, courant, load_sem.at[1]),
+        pltpu.make_async_copy(state_ref, state.at[pl.ds(0, ROWS * X)], load_sem.at[0]),
+        pltpu.make_async_copy(courant_ref, courant.at[pl.ds(0, 2 * LEV * X)], load_sem.at[1]),
         pltpu.make_async_copy(col_in, col_ref, load_sem.at[2]),
         pltpu.make_async_copy(lev_in, lev_ref, load_sem.at[3]),
         pltpu.make_async_copy(innov_in, innov_ref, load_sem.at[4]),
@@ -263,7 +263,7 @@
         pick_copies.append(copy)
     held[me, :LOCAL] = pick_for(me)
     lax.fori_loop(0, X, pack, 0, unroll=4)
-    outs.append(pltpu.make_async_copy(field, field_out, out_sem.at[0]))
+    outs.append(pltpu.make_async_copy(field.at[pl.ds(0, ROWS * X)], field_out, out_sem.at[0]))
     outs[1].start()
     for copy in pick_copies:
         copy.wait_recv()
@@ -599,13 +599,13 @@
         in_specs=[ANY] * 6,
         out_specs=[ANY, ANY, ANY],
         scratch_shapes=[
-            pltpu.VMEM((ROWS * X, CY), f32),
-            pltpu.VMEM((2 * LEV * X, CY), f32),
+            pltpu.VMEM((ROWS * X + X, CY), f32),
+            pltpu.VMEM((2 * LEV * X + X, CY), f32),
             pltpu.VMEM((X + 4, ROWS, CY), f32),
             pltpu.VMEM((X + 2, ROWS, CY), f32),
             pltpu.VMEM((X, ROWS, CY), f32),
             pltpu.VMEM((X + 2, 2 * LEV, CY), f32),
-            pltpu.VMEM((ROWS * X, CY), f32),
+            pltpu.VMEM((ROWS * X + X, CY), f32),
             pltpu.VMEM((1, NOBS), jnp.int32),
             pltpu.VMEM((1, NOBS), jnp.int32),
             pltpu.VMEM((1, NOBS), f32),

time: 58.8 us -> 59.5 us (1.012); the launches traced: 58.7 us -> 58.7 us
  no operation moved by 1% of the time
where the time goes in v6:
time: 59.5 us; the launch traced here: 58.7 us
  Pallas kernels  57.4 us (96%)
  between operations  0.67 us (1%)
  local copies, waits for them, and re-layouts  0.63 us (1%)
    pallas_call x1, Pallas kernels, on_device(): pl.pallas_call(functools.partial(front, plane, depth, piece), out_shape=[...  38.7 us
    pallas_call x1, Pallas kernels, on_device(): pl.pallas_call(functools.partial(solve, piece), out_shape=[jax.ShapeDtype...  13.7 us
    pallas_call x1, Pallas kernels, on_device(): pl.pallas_call(finish, out_shape=jax.ShapeDtypeStruct((LEV, RUN * CY), f3...  5.01 us

profile of v6, /device:TPU:1, one launch (start us, length us, event | category | flops | bytes accessed | tf_op | source)
XLA Modules:
  0.0 58.7 jit_solution(16685845402071939442)
XLA Ops:
  0.6 0.0 copy-start
  0.6 38.7 %front.1 = (f32[3840,128]{1,0:T(8,128)}, f32[24,160,128]{2,1,0:T(8,128)}, f32[256,16,128]{2,1,0:T(8,128)}) custom-call(f32[3840,128]{1,0:T(8,128)} %bitcast.7, f32[768,128]{1,0:T(8,128)} %bitcast.8, s32[1,512]{1,0:T(1,128)} %bitcast.9, s32[1,512]{1,0:T(1,128)} %bitcast.10, f32[1,512]{1,0:T(1,128)} %bitcast.11, f32[1,512]{1,0:T(1,128)} %bitcast.12), custom_call_target="tpu_custom_call" | custom-call | tf_op jit(solution)/shard_map/front/pallas_call | solution.py:592
  39.3 0.0 copy-done
  39.3 13.7 %solve.1 = (f32[10,16,128]{2,1,0:T(8,128)S(1)}, f32[3840,128]{1,0:T(8,128)}) custom-call(f32[256,16,128]{2,1,0:T(8,128)} %get-tuple-element.7.sums_in, s32[12]{0:T(128)S(1)} %copy-done, f32[3840,128]{1,0:T(8,128)} %get-tuple-element.8.field_ref), custom_call_target="tpu_custom_call" | custom-call | tf_op jit(solution)/shard_map/solve/pallas_call | solution.py:651
  53.0 5.0 %finish.1 = f32[16,768]{1,0:T(8,128)S(1)} custom-call(f32[10,16,128]{2,1,0:T(8,128)S(1)} %get-tuple-element.10.coeff_in, f32[24,160,128]{2,1,0:T(8,128)} %get-tuple-element.11.rows_ref), custom_call_target="tpu_custom_call" | custom-call | tf_op jit(solution)/shard_map/finish/pallas_call | solution.py:672
  58.0 0.6 %copy.10 = f32[16,768]{1,0:T(8,128)} copy(f32[16,768]{1,0:T(8,128)S(1)} %finish.1) | data formatting | bytes 98304
Async XLA Ops:
  0.6 38.7 %copy-start = (s32[12]{0:T(128)S(1)}, s32[12]{0:T(128)}, u32[]{:S(2)}) copy-start(s32[12]{0:T(128)} %waves_ref.1) | copy-start | bytes 148
